TPU v7x, 512 devices: a whole 4x4x16 slice. The times are simulated.
512 devices in a mesh: row: 64 (over z, y), col: 8 (over x, core).
Axes of the slice: x: 4, y: 4, z: 16, core: 2. Of those that a mesh axis runs over, the one named last changes fastest.
Arguments:
- panel: float32 [65536, 512], P(('row', 'col')), may hold values from -1.2 to 1.2
- inverse_factor: float32 [512, 512], replicated, as said below
- slab: bfloat16 [65536, 8192], P('row', 'col'), may hold values from -6 to 6
Outputs:
- factor_panel: bfloat16 [65536, 512], P(('row', 'col'))
- updated_slab: bfloat16 [65536, 8192], P('row', 'col')
Inputs may be any that keep to these rules, and one draw needn't show every extreme that they name: `inverse_factor`: lower triangular with a positive diagonal.
All inputs are finite; a program needn't handle non-finite values.
Results may differ from a plain program's by a relative error of at most 0.0052.
Values may be sent and summed in bfloat16 or wider, within the bound.
No kernel may reach another device: no remote copies, remote signals or barrier semaphores. Data moves between devices by JAX's collectives and lax.ppermute only.
A program may use at most 64 MiB of HBM per device.

v0:
```python
import jax
import jax.numpy as jnp
from jax import lax
from jax.sharding import PartitionSpec as P

TILE = 128


def broadcast(value, axis, source):
    kept = jnp.where(lax.axis_index(axis) == source, value, 0).astype(value.dtype)
    return lax.psum(kept, axis)


def solve_panel(rows, inverse_factor):
    return lax.dot_general(
        rows,
        inverse_factor,
        (((1,), (1,)), ((), ())),
        precision=lax.Precision.HIGHEST,
        preferred_element_type=jnp.float32,
    ).astype(jnp.bfloat16)


def times_mirror(factor_rows, mirror_rows):
    return lax.dot_general(
        factor_rows, mirror_rows, (((1,), (1,)), ((), ())), preferred_element_type=jnp.float32
    )


def shards(panel, inverse_factor, slab):
    col_count = lax.axis_size("col")
    row_count = lax.axis_size("row")
    my_col = lax.axis_index("col")
    own_factor = solve_panel(panel, inverse_factor)
    factor_rows = lax.all_gather(own_factor, "col", axis=0, tiled=True)
    leading_tile = factor_rows[:TILE]
    turns = row_count // col_count
    blocks = []
    for turn in range(turns):
        root_row = turn * col_count + my_col
        mirror_tile = broadcast(leading_tile, "row", root_row)
        slab_block = slab[:, turn * TILE : (turn + 1) * TILE].astype(jnp.float32)
        blocks.append((slab_block - times_mirror(factor_rows, mirror_tile)).astype(jnp.bfloat16))
    updated_slab = jnp.concatenate(blocks, axis=1)
    return (own_factor, updated_slab)


def solution(mesh):
    return jax.shard_map(
        shards,
        mesh=mesh,
        in_specs=(P(("row", "col"), None), P(), P("row", "col")),
        out_specs=(P(("row", "col"), None), P("row", "col")),
        check_vma=False,
    )
```

profile of v0, /device:TPU:6, one launch (start us, length us, event | category | flops | bytes accessed | tf_op | source)
XLA Modules:
  0.0 347.6 jit_solution(17573661180240331980)
XLA Ops:
  7.2 0.0 copy-start
  7.2 0.0 copy-start.2
  7.2 0.0 all-gather.2.cloned.1.call-start
  7.2 1.2 copy-done
  8.4 2.8 convolution_convert_fusion
  11.2 0.0 all-gather.2.cloned.1.call-update
  11.2 0.0 all-reduce.3.cloned.1.call-start
  11.3 34.3 %all-gather.2.cloned.1.call-done = bf16[1024,512]{1,0:T(8,128)(2,1)} async-done(((bf16[128,512]{1,0:T(8,128)(2,1)}), bf16[1024,512]{1,0:T(8,128)(2,1)}) %all-gather.2.cloned.1.call-update) | async-done | bytes 1048592 | tf_op jit(solution)/shard_map/all_gather | solution.py:35
  45.5 1.9 broadcast_select_fusion
  47.5 0.0 all-reduce.3.cloned.1.call-update
  47.5 0.0 copy-done.2
  47.5 1.4 fusion.16
  48.9 0.0 copy-start.5
  48.9 0.0 copy-start.4
  48.9 1.2 copy.21
  50.1 1.8 copy.20
  51.9 1.8 copy.19
  53.7 1.8 copy.18
  55.5 0.0 copy-done.5
  55.5 0.9 copy.17
  56.3 0.0 copy-done.4
  56.4 0.8 copy.16
  57.2 0.0 copy-done.3
  57.2 0.1 copy.15
  57.4 0.0 copy-start.10
  57.4 0.1 copy.14
  57.5 267.9 %all-reduce.3.cloned.1.call-done = (bf16[128,512]{1,0:T(8,128)(2,1)}, bf16[128,512]{1,0:T(8,128)(2,1)}, bf16[128,512]{1,0:T(8,128)(2,1)}, bf16[128,512]{1,0:T(8,...) async-done(((bf16[128,512]{1,0:T(8,128)(2,1)}, bf16[128,512]{1,0:T(8,128)(2,1)}, ...) | async-done | bytes 1048592 | tf_op jit(solution)/shard_map/psum | solution.py:11
  325.4 0.0 copy-done.1
  325.4 2.1 fusion.1
  327.5 2.1 fusion.3
  329.7 0.0 copy-done.10
  329.7 0.0 copy-done.16
  329.7 1.2 fusion.5
  330.9 0.0 copy-done.9
  330.9 0.0 copy-done.15
  330.9 1.2 fusion.7
  332.1 0.0 copy-done.8
  332.1 0.0 copy-done.14
  332.1 1.2 fusion.9
  333.3 0.0 copy-done.7
  333.3 0.0 copy-done.13
  333.3 1.2 fusion.11
  334.5 0.0 copy-done.6
  334.5 0.0 copy-done.12
  334.5 1.2 fusion.13
  335.7 0.0 copy-done.11
  335.7 1.2 fusion.15
  336.9 3.9 %copy.13 = bf16[1024,1024]{1,0:T(8,128)(2,1)} copy(bf16[1024,1024]{0,1:T(8,128)(2,1)} %fusion.15) | data formatting | bytes 4194304
  (12 shorter events, 0.0 us)
Async XLA Ops:
  7.2 1.2 copy-start
  7.2 40.3 %copy-start.2 = (bf16[1024,1024]{1,0:T(8,128)(2,1)S(1)}, bf16[1024,1024]{1,0:T(8,128)(2,1)}, u32[]{:S(2)}) copy-start(bf16[1024,1024]{1,0:T(8,128)(2,1)} %param.5) | copy-start | bytes 6291460
  7.2 38.4 %all-gather.2.cloned.1.call-start = ((), (), s32[]{:S(2)}) async-start(), calls=%async_computation | async-start | bytes 1179648 | tf_op jit(solution)/shard_map/all_gather | solution.py:35
  11.2 314.2 %all-reduce.3.cloned.1.call-start = ((), (), s32[]{:S(2)}) async-start(), calls=%async_computation.1 | async-start | bytes 2097152 | tf_op jit(solution)/shard_map/psum | solution.py:11
  48.9 6.6 %copy-start.5 = (bf16[1024,128]{1,0:T(8,128)(2,1)S(1)}, bf16[1024,128]{1,0:T(8,128)(2,1)}, u32[]{:S(2)}) copy-start(bf16[1024,128]{1,0:T(8,128)(2,1)} %get-tuple-element.16) | copy-start | bytes 786436
  48.9 7.5 %copy-start.4 = (bf16[1024,128]{1,0:T(8,128)(2,1)S(1)}, bf16[1024,128]{1,0:T(8,128)(2,1)}, u32[]{:S(2)}) copy-start(bf16[1024,128]{1,0:T(8,128)(2,1)} %get-tuple-element.17) | copy-start | bytes 786436
  48.9 8.3 %copy-start.3 = (bf16[1024,128]{1,0:T(8,128)(2,1)S(1)}, bf16[1024,128]{1,0:T(8,128)(2,1)}, u32[]{:S(2)}) copy-start(bf16[1024,128]{1,0:T(8,128)(2,1)} %get-tuple-element.18) | copy-start | bytes 786436
  48.9 276.5 %copy-start.1 = (bf16[1024,512]{1,0:T(8,128)(2,1)S(1)}, bf16[1024,512]{1,0:T(8,128)(2,1)}, u32[]{:S(2)}) copy-start(bf16[1024,512]{1,0:T(8,128)(2,1)} %all-gather.2.cloned.1.call-done) | copy-start | bytes 3145732
  57.4 272.3 %copy-start.10 = (bf16[1024,128]{0,1:T(8,128)(2,1)S(1)}, bf16[1024,128]{0,1:T(8,128)(2,1)}, u32[]{:S(2)}) copy-start(bf16[1024,128]{0,1:T(8,128)(2,1)} %copy.16) | copy-start | bytes 786436
  325.4 4.3 %copy-start.16 = (bf16[128,512]{1,0:T(8,128)(2,1)S(1)}, bf16[128,512]{1,0:T(8,128)(2,1)}, u32[]{:S(2)}) copy-start(bf16[128,512]{1,0:T(8,128)(2,1)} %get-tuple-element.6) | copy-start | bytes 393220
  327.5 3.4 copy-start.9
  327.5 3.4 copy-start.15
  329.7 2.4 copy-start.8
  329.7 2.4 copy-start.14
  330.9 2.4 copy-start.7
  330.9 2.4 copy-start.13
  332.1 2.4 copy-start.6
  332.1 2.4 copy-start.12
  333.3 2.4 copy-start.11
Sparse Core Ops, SparseCore 0:
  11.3 34.1 all-gather.1
  49.8 275.5 all-reduce.2
where the time goes:
time: 348 us
  waiting for transfers between devices  302 us (87%)
  local copies, waits for them, and re-layouts  15.1 us (4%)
  matrix products  14.2 us (4%)
  between operations  14.1 us (4%)
    psum x1, waiting for transfers between devices, broadcast(): return lax.psum(kept, axis)  268 us
    all_gather x1, waiting for transfers between devices, shards(): factor_rows = lax.all_gather(own_factor, 'col', axis=0, tiled=True)  34.3 us
    unnamed x43, local copies, waits for them, and re-layouts  13.8 us
    dot_general x8, matrix products, times_mirror(): lax.dot_general(factor_rows, mirror_rows, (((1,), (1,)), ((), ())), prefe...  11.4 us
  transfers between devices with their start and end apart: 2, of which 2 were waited for; matrix products, arithmetic and copies ran while one was open for 3% of the time, Pallas kernels for 0%

commit v1 on v0

v1 whole, which is shorter than its diff:
```python
import jax
import jax.numpy as jnp
from jax import lax
from jax.sharding import PartitionSpec as P

TILE = 128
ROWS = 64
COLS = 8
PIECE = TILE // COLS
Y = 4
Z = 16
Y_GROUPS = [[z * Y + y for y in range(Y)] for z in range(Z)]
Z_GROUPS = [[z * Y + y for z in range(Z)] for y in range(Y)]
MESH_AXES = ("row", "col")


def device(row, col):
    return row * COLS + col


def permute(value, target):
    return lax.ppermute(
        value,
        MESH_AXES,
        [(device(r, c), device(*target(r, c))) for r in range(ROWS) for c in range(COLS)],
    )


def solve_panel(rows, inverse_factor):
    return lax.dot_general(
        rows,
        inverse_factor,
        (((1,), (1,)), ((), ())),
        precision=lax.Precision.HIGHEST,
        preferred_element_type=jnp.float32,
    ).astype(jnp.bfloat16)


def spread(value, axis, groups, count):
    copies = jnp.broadcast_to(value[None], (count,) + value.shape)
    return lax.all_to_all(copies, axis, 0, 0, axis_index_groups=groups, tiled=True)


def shards(panel, inverse_factor, slab):
    own_factor = solve_panel(panel, inverse_factor)
    pieces = lax.all_to_all(
        own_factor.reshape(COLS, PIECE, -1), "col", 0, 0, tiled=True
    )
    piece = permute(pieces[0], lambda r, c: (r // COLS * COLS + c, r % COLS))
    along_z = spread(piece, "row", Z_GROUPS, Z)
    blocks = [own_factor] + [
        permute(own_factor, lambda r, c, k=k: (r, (c + 2 * k) % COLS)) for k in (1, 2, 3)
    ]
    mine = jnp.stack(blocks)
    other = permute(mine, lambda r, c: (r, c ^ 1))
    my_col = lax.axis_index("col")
    core = my_col % 2
    pair = jnp.where(core == 0, jnp.stack([mine, other], 1), jnp.stack([other, mine], 1))
    x = my_col // 2
    order = (x - jnp.arange(4)) % 4
    factor_rows = pair[order].reshape(COLS * TILE, -1)
    along_y = spread(along_z, "row", Y_GROUPS, Y)
    mirror = along_y.reshape(Y, 8, 2, PIECE, -1).transpose(1, 2, 0, 3, 4).reshape(8 * TILE, -1)
    product = lax.dot_general(
        factor_rows, mirror, (((1,), (1,)), ((), ())), preferred_element_type=jnp.float32
    )
    return own_factor, (slab.astype(jnp.float32) - product).astype(jnp.bfloat16)


def solution(mesh):
    return jax.shard_map(
        shards,
        mesh=mesh,
        in_specs=(P(("row", "col"), None), P(), P("row", "col")),
        out_specs=(P(("row", "col"), None), P("row", "col")),
        check_vma=False,
    )
```

time: 348 us -> 80.9 us (0.23)
  the two profiles are of different devices: /device:TPU:6 before, /device:TPU:32 now
where the time goes in v1:
time: 80.9 us; the launch traced here: 80.3 us
  starting transfers between devices  37.8 us (47%)
  waiting for transfers between devices  16.9 us (21%)
  blocking collectives  10.2 us (13%)
  matrix products  6.34 us (8%)
  local copies, waits for them, and re-layouts  5.55 us (7%)
  other arithmetic  2.7 us (3%)
    all_to_all x2, starting transfers between devices, spread(): lax.all_to_all(copies, axis, 0, 0, axis_index_groups=groups, tiled=True)  19.7 us
    ppermute x5, starting transfers between devices, permute(): lax.ppermute(value, MESH_AXES, [(device(r, c), device(*target(r, c))) for...  18.1 us
    all_to_all x2, waiting for transfers between devices, spread(): lax.all_to_all(copies, axis, 0, 0, axis_index_groups=groups, tiled=True)  13 us
    all_to_all x1, blocking collectives, shards(): lax.all_to_all(own_factor.reshape(COLS, PIECE, -1), 'col', 0, 0, tiled=True)  10.2 us
    dot_general x1, matrix products, shards(): lax.dot_general(factor_rows, mirror, (((1,), (1,)), ((), ())), preferred_...  4.22 us
    ppermute x5, waiting for transfers between devices, permute(): lax.ppermute(value, MESH_AXES, [(device(r, c), device(*target(r, c))) for...  3.92 us
    dot_general x1, matrix products, solve_panel(): lax.dot_general(rows, inverse_factor, (((1,), (1,)), ((), ())), precision...  2.12 us
    unnamed x8, local copies, waits for them, and re-layouts  2.06 us
  transfers between devices with their start and end apart: 7, of which 4 were waited for; matrix products, arithmetic and copies ran while one was open for 7% of the time, Pallas kernels for 0%

profile of v1, /device:TPU:32, one launch (start us, length us, event | category | flops | bytes accessed | tf_op | source)
XLA Modules:
  0.0 80.3 jit_solution(17509000123010346038)
XLA Ops:
  0.6 0.0 copy-start
  0.6 1.2 %copy-done = f32[512,512]{1,0:T(8,128)S(1)} copy-done((f32[512,512]{1,0:T(8,128)S(1)}, f32[512,512]{1,0:T(8,128)}, u32[]{:S(2)}) %copy-start) | copy-done | bytes 1048600
  1.9 2.1 %convolution_convert_fusion = bf16[128,512]{1,0:T(8,128)(2,1)S(1)} fusion(f32[128,512]{1,0:T(8,128)} %param.3, f32[512,512]{1,0:T(8,128)S(1)} %copy-done), kind=kOutput, calls=%fused_computation.2 | convolution fusion | flops 402718720 | bytes 1441792 | tf_op jit(solution)/shard_map/dot_general | solution.py:30
  4.0 0.0 copy-start.1
  4.0 10.2 %all_to_all.15 = bf16[8,16,512]{2,1,0:T(8,128)(2,1)S(1)} all-to-all(bf16[8,16,512]{2,1,0:T(8,128)(2,1)S(1)} %bitcast.22), channel_id=1, replica_groups=mesh['row'=64,'col'=8] {'col'}, dimensions={0} | all-to-all | bytes 262144 | tf_op jit(solution)/shard_map/all_to_all | solution.py:46
  14.2 5.9 %collective-permute-start.4 = (bf16[16,512]{1,0:T(8,128)(2,1)S(1)}, bf16[16,512]{1,0:T(8,128)(2,1)S(1)}, u32[]{:S(2)}, u32[]{:S(2)}) collective-permute-start(bf16[16,512]{1,0:T(8,128)(2,1)S(1)} %slice_bitcast_fusion), channel_id=1, source_target_pairs={{0,0},{1,8},{2,16},{3,24},{4,32},{5,40},{6,48},{7,56},{8,1},{9,9},... | collective-permute-start | bytes 49160 | tf_op jit(solution)/shard_map/ppermute | solution.py:22
  20.2 2.1 %collective-permute-done.4 = bf16[16,512]{1,0:T(8,128)(2,1)S(1)} collective-permute-done((bf16[16,512]{1,0:T(8,128)(2,1)S(1)}, bf16[16,512]{1,0:T(8,128)(2,1)S(1)}, u32[]{:S(2)}, u32[]{:S(2)}) %collective-permute-start.4) | collective-permute-done | bytes 16416 | tf_op jit(solution)/shard_map/ppermute | solution.py:22
  22.3 0.7 broadcast_in_dim.4
  23.0 14.8 %all-to-all-start.1 = ((bf16[16,16,512]{2,1,0:T(8,128)(2,1)}), bf16[16,16,512]{2,1,0:T(8,128)(2,1)S(1)}, u32[]{:S(2)}, u32[]{:S(2)}) async-start(bf16[16,16,512]{2,1,0:T(8,128)(2,1)} %broadcast_in_dim.4), calls=%async_computation.1 | async-start | bytes 524288 | tf_op jit(solution)/shard_map/all_to_all | solution.py:41
  37.8 5.6 %collective-permute-start.2 = (bf16[128,512]{1,0:T(8,128)(2,1)S(1)}, bf16[128,512]{1,0:T(8,128)(2,1)S(1)}, u32[]{:S(2)}, u32[]{:S(2)}) collective-permute-start(bf16[128,512]{1,0:T(8,128)(2,1)S(1)} %convolution_convert_fusion), channel_id=1, source_target_pairs={{0,6},{1,7},{2,0},{3,1},{4,2},{5,3},{6,4},{7,5},{8,14},{9,15},{10,... | collective-permute-start | bytes 393224 | tf_op jit(solution)/shard_map/ppermute | solution.py:22
  43.4 1.9 %collective-permute-start.1 = (bf16[128,512]{1,0:T(8,128)(2,1)S(1)}, bf16[128,512]{1,0:T(8,128)(2,1)S(1)}, u32[]{:S(2)}, u32[]{:S(2)}) collective-permute-start(bf16[128,512]{1,0:T(8,128)(2,1)S(1)} %convolution_convert_fusion), channel_id=1, source_target_pairs={{0,4},{1,5},{2,6},{3,7},{4,0},{5,1},{6,2},{7,3},{8,12},{9,13},{10,... | collective-permute-start | bytes 393224 | tf_op jit(solution)/shard_map/ppermute | solution.py:22
  45.3 2.8 %collective-permute-start = (bf16[128,512]{1,0:T(8,128)(2,1)S(1)}, bf16[128,512]{1,0:T(8,128)(2,1)S(1)}, u32[]{:S(2)}, u32[]{:S(2)}) collective-permute-start(bf16[128,512]{1,0:T(8,128)(2,1)S(1)} %convolution_convert_fusion), channel_id=1, source_target_pairs={{0,2},{1,3},{2,4},{3,5},{4,6},{5,7},{6,0},{7,1},{8,10},{9,11},{10,... | collective-permute-start | bytes 393224 | tf_op jit(solution)/shard_map/ppermute | solution.py:22
  48.1 7.9 %all-to-all-done.1 = bf16[16,16,512]{2,1,0:T(8,128)(2,1)S(1)} async-done(((bf16[16,16,512]{2,1,0:T(8,128)(2,1)}), bf16[16,16,512]{2,1,0:T(8,128)(2,1)S(1)}, u32[]{:S(2)}, u32[]{:S(2)}) %all-to-all-start.1) | async-done | bytes 262176 | tf_op jit(solution)/shard_map/all_to_all | solution.py:41
  56.0 1.1 %broadcast_in_dim.5 = bf16[4,16,16,512]{3,2,1,0:T(8,128)(2,1)} broadcast(bf16[16,16,512]{2,1,0:T(8,128)(2,1)S(1)} %all-to-all-done.1), dimensions={1,2,3} | broadcast | bytes 1310720 | tf_op jit(solution)/shard_map/broadcast_in_dim | solution.py:40
  57.1 4.9 %all-to-all-start.2 = ((bf16[4,16,16,512]{3,2,1,0:T(8,128)(2,1)}), bf16[4,16,16,512]{3,2,1,0:T(8,128)(2,1)S(1)}, u32[]{:S(2)}, u32[]{:S(2)}) async-start(bf16[4,16,16,512]{3,2,1,0:T(8,128)(2,1)} %broadcast_in_dim.5), calls=%async_computation.2 | async-start | bytes 2097152 | tf_op jit(solution)/shard_map/all_to_all | solution.py:41
  62.0 0.0 collective-permute-done.2
  62.0 0.0 collective-permute-done.1
  62.0 0.0 collective-permute-done
  62.0 0.0 copy-done.1
  62.0 0.9 %fusion.2 = (bf16[4,1,128,512]{3,2,0,1:T(8,128)(2,1)}, bf16[4,128,512]{2,1,0:T(8,128)(2,1)S(1)}) fusion(bf16[1,128,512]{2,1,0:T(8,128)(2,1)S(1)} %bitcast.27, bf16[1,128,512]{2,1,0:T(8,128)(2,1)S(1)} %bitcast.28, bf16[1,128,512]{2,1,0:T(8,128)(2,1)S(1)} %bitcast.29, bf16[1,128,512]{2,1,0:T(8,128)(2,1)S(1)} %bitcast.23), kind=kLoop, calls=%fused_computation.13 | loop fusion | flops 786432 | bytes 1572864 | tf_op jit(solution)/shard_map/stack | solution.py:58
  62.9 1.9 %collective-permute-start.3 = (bf16[4,128,512]{2,1,0:T(8,128)(2,1)S(1)}, bf16[4,128,512]{2,1,0:T(8,128)(2,1)S(1)}, u32[]{:S(2)}, u32[]{:S(2)}) collective-permute-start(bf16[4,128,512]{2,1,0:T(8,128)(2,1)S(1)} %get-tuple-element.3), channel_id=1, source_target_pairs={{0,1},{1,0},{2,3},{3,2},{4,5},{5,4},{6,7},{7,6},{8,9},{9,8},{10,11... | collective-permute-start | bytes 1572872 | tf_op jit(solution)/shard_map/ppermute | solution.py:22
  64.9 1.8 %collective-permute-done.3 = bf16[4,128,512]{2,1,0:T(8,128)(2,1)S(1)} collective-permute-done((bf16[4,128,512]{2,1,0:T(8,128)(2,1)S(1)}, bf16[4,128,512]{2,1,0:T(8,128)(2,1)S(1)}, u32[]{:S(2)}, u32[]{:S(2)}) %collective-permute-start.3) | collective-permute-done | bytes 524320 | tf_op jit(solution)/shard_map/ppermute | solution.py:22
  66.7 0.0 copy-start.3
  66.7 0.8 %copy-done.3 = bf16[4,128,512]{2,1,0:T(8,128)(2,1)} copy-done((bf16[4,128,512]{2,1,0:T(8,128)(2,1)}, bf16[4,128,512]{2,1,0:T(8,128)(2,1)S(1)}, u32[]{:S(2)}) %copy-start.3) | copy-done | bytes 524312
  67.6 1.8 %maximum_select_fusion = bf16[4,2,128,512]{3,2,0,1:T(8,128)(2,1)S(1)} fusion(bf16[4,1,128,512]{3,2,0,1:T(8,128)(2,1)} %bitcast.26, bf16[4,1,128,512]{3,2,0,1:T(8,128)(2,1)} %get-tuple-element.2, pred[]{:T(512)S(6)} %eq.7), kind=kLoop, calls=%fused_computation.3 | loop fusion | flops 1572864 | bytes 2097153 | tf_op jit(solution)/shard_map/jit(_where)/select_n | solution.py:58
  69.4 1.6 %gather_fusion = bf16[4,2,128,512]{3,2,1,0:T(8,128)(2,1)} fusion(bf16[4,2,128,512]{3,2,0,1:T(8,128)(2,1)S(1)} %maximum_select_fusion, s32[1024]{0:T(1024)S(1)} %pad_clamp_fusion), kind=kCustom, calls=%fused_computation | custom fusion | bytes 2097168 | tf_op jit(solution)/shard_map/gather | solution.py:61
  70.9 0.0 copy-start.2
  70.9 5.1 %all-to-all-done.2 = bf16[4,16,16,512]{3,2,1,0:T(8,128)(2,1)S(1)} async-done(((bf16[4,16,16,512]{3,2,1,0:T(8,128)(2,1)}), bf16[4,16,16,512]{3,2,1,0:T(8,128)(2,1)S(1)}, u32[]{:S(2)}, u32[]{:S(2)}) %all-to-all-start.2) | async-done | bytes 1048608 | tf_op jit(solution)/shard_map/all_to_all | solution.py:41
  76.0 0.1 copy.5
  76.1 0.0 copy-done.2
  76.1 4.2 %subtract_convert_fusion = bf16[1024,1024]{1,0:T(8,128)(2,1)} fusion(bf16[1024,1024]{1,0:T(8,128)(2,1)} %param.5, bf16[1024,512]{1,0:T(8,128)(2,1)S(1)} %bitcast.24, bf16[1024,512]{1,0:T(8,128)(2,1)S(1)} %bitcast.25), kind=kOutput, calls=%fused_computation.1 | convolution fusion | flops 1076887552 | bytes 6291456 | tf_op jit(solution)/shard_map/dot_general | solution.py:64
  (3 shorter events, 0.0 us)
Async XLA Ops:
  0.6 1.2 %copy-start = (f32[512,512]{1,0:T(8,128)S(1)}, f32[512,512]{1,0:T(8,128)}, u32[]{:S(2)}) copy-start(f32[512,512]{1,0:T(8,128)} %param.4) | copy-start | bytes 3145732
  4.0 58.1 %copy-start.1 = (bf16[128,512]{1,0:T(8,128)(2,1)}, bf16[128,512]{1,0:T(8,128)(2,1)S(1)}, u32[]{:S(2)}) copy-start(bf16[128,512]{1,0:T(8,128)(2,1)S(1)} %convolution_convert_fusion) | copy-start | bytes 393220
  14.2 8.0 %collective-permute-start.4 = (bf16[16,512]{1,0:T(8,128)(2,1)S(1)}, bf16[16,512]{1,0:T(8,128)(2,1)S(1)}, u32[]{:S(2)}, u32[]{:S(2)}) collective-permute-start(bf16[16,512]{1,0:T(8,128)(2,1)S(1)} %slice_bitcast_fusion), channel_id=1, source_target_pairs={{0,0},{1,8},{2,16},{3,24},{4,32},{5,40},{6,48},{7,56},{8,1},{9,9},... | collective-permute-start | bytes 49160 | tf_op jit(solution)/shard_map/ppermute | solution.py:22
  23.0 33.0 %all-to-all-start.1 = ((bf16[16,16,512]{2,1,0:T(8,128)(2,1)}), bf16[16,16,512]{2,1,0:T(8,128)(2,1)S(1)}, u32[]{:S(2)}, u32[]{:S(2)}) async-start(bf16[16,16,512]{2,1,0:T(8,128)(2,1)} %broadcast_in_dim.4), calls=%async_computation.1 | async-start | bytes 524288 | tf_op jit(solution)/shard_map/all_to_all | solution.py:41
  37.8 24.3 %collective-permute-start.2 = (bf16[128,512]{1,0:T(8,128)(2,1)S(1)}, bf16[128,512]{1,0:T(8,128)(2,1)S(1)}, u32[]{:S(2)}, u32[]{:S(2)}) collective-permute-start(bf16[128,512]{1,0:T(8,128)(2,1)S(1)} %convolution_convert_fusion), channel_id=1, source_target_pairs={{0,6},{1,7},{2,0},{3,1},{4,2},{5,3},{6,4},{7,5},{8,14},{9,15},{10,... | collective-permute-start | bytes 393224 | tf_op jit(solution)/shard_map/ppermute | solution.py:22
  43.4 18.6 %collective-permute-start.1 = (bf16[128,512]{1,0:T(8,128)(2,1)S(1)}, bf16[128,512]{1,0:T(8,128)(2,1)S(1)}, u32[]{:S(2)}, u32[]{:S(2)}) collective-permute-start(bf16[128,512]{1,0:T(8,128)(2,1)S(1)} %convolution_convert_fusion), channel_id=1, source_target_pairs={{0,4},{1,5},{2,6},{3,7},{4,0},{5,1},{6,2},{7,3},{8,12},{9,13},{10,... | collective-permute-start | bytes 393224 | tf_op jit(solution)/shard_map/ppermute | solution.py:22
  45.3 16.7 %collective-permute-start = (bf16[128,512]{1,0:T(8,128)(2,1)S(1)}, bf16[128,512]{1,0:T(8,128)(2,1)S(1)}, u32[]{:S(2)}, u32[]{:S(2)}) collective-permute-start(bf16[128,512]{1,0:T(8,128)(2,1)S(1)} %convolution_convert_fusion), channel_id=1, source_target_pairs={{0,2},{1,3},{2,4},{3,5},{4,6},{5,7},{6,0},{7,1},{8,10},{9,11},{10,... | collective-permute-start | bytes 393224 | tf_op jit(solution)/shard_map/ppermute | solution.py:22
  57.1 18.9 %all-to-all-start.2 = ((bf16[4,16,16,512]{3,2,1,0:T(8,128)(2,1)}), bf16[4,16,16,512]{3,2,1,0:T(8,128)(2,1)S(1)}, u32[]{:S(2)}, u32[]{:S(2)}) async-start(bf16[4,16,16,512]{3,2,1,0:T(8,128)(2,1)} %broadcast_in_dim.5), calls=%async_computation.2 | async-start | bytes 2097152 | tf_op jit(solution)/shard_map/all_to_all | solution.py:41
  62.9 3.8 %collective-permute-start.3 = (bf16[4,128,512]{2,1,0:T(8,128)(2,1)S(1)}, bf16[4,128,512]{2,1,0:T(8,128)(2,1)S(1)}, u32[]{:S(2)}, u32[]{:S(2)}) collective-permute-start(bf16[4,128,512]{2,1,0:T(8,128)(2,1)S(1)} %get-tuple-element.3), channel_id=1, source_target_pairs={{0,1},{1,0},{2,3},{3,2},{4,5},{5,4},{6,7},{7,6},{8,9},{9,8},{10,11... | collective-permute-start | bytes 1572872 | tf_op jit(solution)/shard_map/ppermute | solution.py:22
  66.7 0.8 %copy-start.3 = (bf16[4,128,512]{2,1,0:T(8,128)(2,1)}, bf16[4,128,512]{2,1,0:T(8,128)(2,1)S(1)}, u32[]{:S(2)}) copy-start(bf16[4,128,512]{2,1,0:T(8,128)(2,1)S(1)} %collective-permute-done.3) | copy-start | bytes 1572868
  70.9 5.1 %copy-start.2 = (bf16[4,2,128,512]{3,2,1,0:T(8,128)(2,1)S(1)}, bf16[4,2,128,512]{3,2,1,0:T(8,128)(2,1)}, u32[]{:S(2)}) copy-start(bf16[4,2,128,512]{3,2,1,0:T(8,128)(2,1)} %gather_fusion) | copy-start | bytes 3145732

commit v2 on v1

v2 whole, which is shorter than its diff:
```python
import jax
import jax.numpy as jnp
from jax import lax
from jax.experimental import pallas as pl
from jax.experimental.pallas import tpu as pltpu
from jax.sharding import PartitionSpec as P

NB = 512
TILE = 128
ROWS = 64
COLS = 8
CHIPS = COLS // 2
PIECE = TILE // COLS
BLOCK = ROWS // COLS
WIDE = 2 * TILE
T_ORDER = [6, 7, 0, 1, 2, 3, 4, 5]
J_ORDER = [4, 5, 6, 7, 0, 1, 2, 3]
APART = [[t * COLS + j for t in T_ORDER] for j in range(COLS)]
NEAR = [[t * COLS + j for j in J_ORDER] for t in range(BLOCK)]
MESH_AXES = ("row", "col")


def device(row, col):
    return row * COLS + col


def permute(value, pairs):
    return lax.ppermute(value, MESH_AXES, [(device(*a), device(*b)) for a, b in pairs])


def everywhere(target):
    return [((r, c), target(r, c)) for r in range(ROWS) for c in range(COLS)]


def solve_panel(rows, inverse_factor):
    return lax.dot_general(
        rows,
        inverse_factor,
        (((1,), (1,)), ((), ())),
        precision=lax.Precision.HIGHEST,
        preferred_element_type=jnp.float32,
    ).astype(jnp.bfloat16)


def spread(value, axis, groups, count):
    copies = jnp.broadcast_to(value[None], (count,) + value.shape)
    return lax.all_to_all(copies, axis, 0, 0, axis_index_groups=groups, tiled=True)


def scatter(tile):
    half = COLS // 2 * PIECE
    taken = permute(tile, [((r, 0), (r, 1)) for r in range(ROWS)])
    part = jnp.where(lax.axis_index("col") == 0, tile[:half], taken[half:])
    total = None
    for j in range(COLS // 2):
        pairs = [
            ((t + c, h), (t + h * (COLS // 2) + j, c))
            for t in range(0, ROWS, COLS)
            for c in range(COLS)
            for h in range(2)
        ]
        got = permute(part[j * PIECE : (j + 1) * PIECE], pairs)
        total = got if total is None else total + got
    return total


def assemble(mine, other):
    my_col = lax.axis_index("col")
    chip, core = my_col // 2, my_col % 2
    pair = jnp.where(core == 0, jnp.stack([mine, other], 1), jnp.stack([other, mine], 1))
    pair = pair.reshape(2, 2, WIDE, NB)
    pair = jnp.where(chip % 2 == 0, pair, pair[:, ::-1])
    pair = jnp.where(chip // 2 == 0, pair, pair[::-1])
    return pair.reshape(COLS * TILE, NB)


def shards(panel, inverse_factor, slab):
    own_factor = solve_panel(panel, inverse_factor)
    one = permute(own_factor, everywhere(lambda r, c: (r, c ^ 2)))
    leading = scatter(panel)
    piece = solve_panel(leading, inverse_factor)
    copies = jnp.broadcast_to(piece[None], (BLOCK, PIECE, NB))
    two = jnp.stack([own_factor, one])
    far = lax.all_to_all(copies, "row", 0, 0, axis_index_groups=APART, tiled=True)
    four = jnp.concatenate([two, permute(two, everywhere(lambda r, c: (r, c ^ 4)))])
    far, four = lax.optimization_barrier((far, four))
    near = spread(far, "row", NEAR, COLS)
    other = permute(four, everywhere(lambda r, c: (r, c ^ 1)))
    factor_rows = assemble(four, other)
    near = near.reshape(COLS, BLOCK, PIECE, NB)
    mirror = jnp.concatenate(
        [near[J_ORDER.index(j), T_ORDER.index(t)] for t in range(BLOCK) for j in range(COLS)]
    )
    product = lax.dot_general(
        factor_rows, mirror, (((1,), (1,)), ((), ())), preferred_element_type=jnp.float32
    )
    return own_factor, (slab.astype(jnp.float32) - product).astype(jnp.bfloat16)


def solution(mesh):
    return jax.shard_map(
        shards,
        mesh=mesh,
        in_specs=(P(("row", "col"), None), P(), P("row", "col")),
        out_specs=(P(("row", "col"), None), P("row", "col")),
        check_vma=False,
    )
```

time: 80.9 us -> 71.3 us (0.88)
  the two profiles are of different devices: /device:TPU:32 before, /device:TPU:6 now
where the time goes in v2:
time: 71.3 us; the launch traced here: 70.4 us
  starting transfers between devices  31.3 us (44%)
  waiting for transfers between devices  27.5 us (39%)
  matrix products  5.75 us (8%)
  local copies, waits for them, and re-layouts  2.98 us (4%)
  other arithmetic  1.59 us (2%)
  between operations  1.36 us (2%)
    ppermute x8, waiting for transfers between devices, permute(): lax.ppermute(value, MESH_AXES, [(device(*a), device(*b)) for a, b in pairs])  17.9 us
    all_to_all x1, starting transfers between devices, shards(): lax.all_to_all(copies, 'row', 0, 0, axis_index_groups=APART, tiled=True)  15.6 us
    ppermute x8, starting transfers between devices, permute(): lax.ppermute(value, MESH_AXES, [(device(*a), device(*b)) for a, b in pairs])  12.1 us
    all_to_all x1, waiting for transfers between devices, spread(): lax.all_to_all(copies, axis, 0, 0, axis_index_groups=groups, tiled=True)  9.57 us
    all_to_all x1, starting transfers between devices, spread(): lax.all_to_all(copies, axis, 0, 0, axis_index_groups=groups, tiled=True)  3.51 us
    dot_general x2, matrix products, solve_panel(): lax.dot_general(rows, inverse_factor, (((1,), (1,)), ((), ())), precision...  3.09 us
    dot_general x1, matrix products, shards(): lax.dot_general(factor_rows, mirror, (((1,), (1,)), ((), ())), preferred_...  2.66 us
  transfers between devices with their start and end apart: 10, of which 4 were waited for; matrix products, arithmetic and copies ran while one was open for 6% of the time, Pallas kernels for 0%

profile of v2, /device:TPU:6, one launch (start us, length us, event | category | flops | bytes accessed | tf_op | source)
XLA Modules:
  0.0 70.4 jit_solution(13352657650116223631)
XLA Ops:
  0.6 0.0 copy-start
  0.6 0.8 %collective-permute-start = (f32[128,512]{1,0:T(8,128)}, f32[128,512]{1,0:T(8,128)S(1)}, u32[]{:S(2)}, u32[]{:S(2)}) collective-permute-start(f32[128,512]{1,0:T(8,128)} %param.3), channel_id=1, source_target_pairs={{0,1},{8,9},{16,17},{24,25},{32,33},{40,41},{48,49},{56,57},{64,65... | collective-permute-start | bytes 786440 | tf_op jit(solution)/shard_map/ppermute | solution.py:28
  1.5 0.0 collective-permute-done
  1.5 0.9 %slice_select_fusion = f32[64,512]{1,0:T(8,128)S(1)} fusion(f32[128,512]{1,0:T(8,128)S(1)} %collective-permute-done, f32[128,512]{1,0:T(8,128)} %param.3, pred[]{:T(512)S(6)} %eq.18), kind=kLoop, calls=%fused_computation.72 | loop fusion | flops 32768 | bytes 393217 | tf_op jit(solution)/shard_map/jit(_where)/select_n | solution.py:53
  2.4 0.7 collective-permute-start.2
  3.1 0.7 collective-permute-start.4
  3.8 0.7 collective-permute-start.3
  4.4 1.3 %collective-permute-start.1 = (f32[16,512]{1,0:T(8,128)S(1)}, f32[16,512]{1,0:T(8,128)S(1)}, u32[]{:S(2)}, u32[]{:S(2)}) collective-permute-start(f32[16,512]{1,0:T(8,128)S(1)} %get-tuple-element.9), channel_id=1, source_target_pairs={{0,0},{1,32},{8,1},{9,33},{16,2},{17,34},{24,3},{25,35},{32,4},{33... | collective-permute-start | bytes 98312 | tf_op jit(solution)/shard_map/ppermute | solution.py:28
  5.7 0.0 copy-done
  5.7 2.1 %convolution_convert_fusion = bf16[128,512]{1,0:T(8,128)(2,1)S(1)} fusion(f32[128,512]{1,0:T(8,128)} %param.3, f32[512,512]{1,0:T(8,128)S(1)} %copy-done), kind=kOutput, calls=%fused_computation.3 | convolution fusion | flops 402718720 | bytes 1441792 | tf_op jit(solution)/shard_map/dot_general | solution.py:36
  7.9 0.0 copy-start.1
  7.9 2.7 %collective-permute-start.5 = (bf16[128,512]{1,0:T(8,128)(2,1)S(1)}, bf16[128,512]{1,0:T(8,128)(2,1)S(1)}, u32[]{:S(2)}, u32[]{:S(2)}) collective-permute-start(bf16[128,512]{1,0:T(8,128)(2,1)S(1)} %convolution_convert_fusion), channel_id=1, source_target_pairs={{0,2},{1,3},{2,0},{3,1},{4,6},{5,7},{6,4},{7,5},{8,10},{9,11},{10,... | collective-permute-start | bytes 393224 | tf_op jit(solution)/shard_map/ppermute | solution.py:28
  10.6 0.0 collective-permute-done.2
  10.6 0.0 collective-permute-done.4
  10.7 0.0 collective-permute-done.3
  10.7 7.1 %collective-permute-done.1 = f32[16,512]{1,0:T(8,128)S(1)} collective-permute-done((f32[16,512]{1,0:T(8,128)S(1)}, f32[16,512]{1,0:T(8,128)S(1)}, u32[]{:S(2)}, u32[]{:S(2)}) %collective-permute-start.1) | collective-permute-done | bytes 32800 | tf_op jit(solution)/shard_map/ppermute | solution.py:28
  17.8 1.0 %convolution_convert_fusion.1 = bf16[16,512]{1,0:T(8,128)(2,1)S(1)} fusion(f32[512,512]{1,0:T(8,128)S(1)} %copy-done, f32[16,512]{1,0:T(8,128)S(1)} %collective-permute-done.4, f32[16,512]{1,0:T(8,128)S(1)} %collective-permute-done.3, f32[16,512]{1,0:T(8,128)S(1)} %collective-permute-done.1, f32[16,512]{1,0:T(8,128)S(1)} %collective-permute-done.2), kind=kOutput, calls=%fused_computation.4 | convolution fusion | flops 50364416 | bytes 1196032 | tf_op jit(solution)/shard_map/dot_general | solution.py:36
  18.7 0.7 broadcast_in_dim.4
  19.4 15.6 %all-to-all-start = ((bf16[8,16,512]{2,1,0:T(8,128)(2,1)}), bf16[8,16,512]{2,1,0:T(8,128)(2,1)S(1)}, u32[]{:S(2)}, u32[]{:S(2)}) async-start(bf16[8,16,512]{2,1,0:T(8,128)(2,1)} %broadcast_in_dim.4), calls=%async_computation | async-start | bytes 262144 | tf_op jit(solution)/shard_map/all_to_all | solution.py:84
  35.1 0.0 collective-permute-done.5
  35.1 3.4 %collective-permute-start.6 = (bf16[2,128,512]{2,1,0:T(8,128)(2,1)S(1)}, bf16[2,128,512]{2,1,0:T(8,128)(2,1)S(1)}, u32[]{:S(2)}, u32[]{:S(2)}) collective-permute-start(bf16[2,128,512]{2,1,0:T(8,128)(2,1)S(1)} %pad_maximum_fusion.1), channel_id=1, source_target_pairs={{0,4},{1,5},{2,6},{3,7},{4,0},{5,1},{6,2},{7,3},{8,12},{9,13},{10,... | collective-permute-start | bytes 786440 | tf_op jit(solution)/shard_map/ppermute | solution.py:28
  38.5 8.9 %collective-permute-done.6 = bf16[2,128,512]{2,1,0:T(8,128)(2,1)S(1)} collective-permute-done((bf16[2,128,512]{2,1,0:T(8,128)(2,1)S(1)}, bf16[2,128,512]{2,1,0:T(8,128)(2,1)S(1)}, u32[]{:S(2)}, u32[]{:S(2)}) %collective-permute-start.6) | collective-permute-done | bytes 262176 | tf_op jit(solution)/shard_map/ppermute | solution.py:28
  47.4 0.1 pad_maximum_fusion
  47.5 0.0 all-to-all-done
  47.5 1.1 %broadcast_in_dim.5 = bf16[8,8,16,512]{3,2,1,0:T(8,128)(2,1)} broadcast(bf16[8,16,512]{2,1,0:T(8,128)(2,1)S(1)} %all-to-all-done), dimensions={1,2,3} | broadcast | bytes 1179648 | tf_op jit(solution)/shard_map/broadcast_in_dim | solution.py:46
  48.6 0.0 copy-done.1
  48.6 3.5 %all-to-all-start.1 = ((bf16[8,8,16,512]{3,2,1,0:T(8,128)(2,1)}), bf16[8,8,16,512]{3,2,1,0:T(8,128)(2,1)S(1)}, u32[]{:S(2)}, u32[]{:S(2)}) async-start(bf16[8,8,16,512]{3,2,1,0:T(8,128)(2,1)} %broadcast_in_dim.5), calls=%async_computation.1 | async-start | bytes 2097152 | tf_op jit(solution)/shard_map/all_to_all | solution.py:47
  52.1 1.9 %collective-permute-start.7 = (bf16[4,128,512]{2,1,0:T(8,128)(2,1)S(1)}, bf16[4,128,512]{2,1,0:T(8,128)(2,1)S(1)}, u32[]{:S(2)}, u32[]{:S(2)}) collective-permute-start(bf16[4,128,512]{2,1,0:T(8,128)(2,1)S(1)} %pad_maximum_fusion), channel_id=1, source_target_pairs={{0,1},{1,0},{2,3},{3,2},{4,5},{5,4},{6,7},{7,6},{8,9},{9,8},{10,11... | collective-permute-start | bytes 1572872 | tf_op jit(solution)/shard_map/ppermute | solution.py:28
  54.1 1.8 %collective-permute-done.7 = bf16[4,128,512]{2,1,0:T(8,128)(2,1)S(1)} collective-permute-done((bf16[4,128,512]{2,1,0:T(8,128)(2,1)S(1)}, bf16[4,128,512]{2,1,0:T(8,128)(2,1)S(1)}, u32[]{:S(2)}, u32[]{:S(2)}) %collective-permute-start.7) | collective-permute-done | bytes 524320 | tf_op jit(solution)/shard_map/ppermute | solution.py:28
  55.9 0.2 maximum_select_fusion
  56.1 0.1 copy.5
  56.2 0.2 reverse_select_fusion.1
  56.4 0.2 reverse_select_fusion
  56.6 9.6 %all-to-all-done.1 = bf16[8,8,16,512]{3,2,1,0:T(8,128)(2,1)S(1)} async-done(((bf16[8,8,16,512]{3,2,1,0:T(8,128)(2,1)}), bf16[8,8,16,512]{3,2,1,0:T(8,128)(2,1)S(1)}, u32[]{:S(2)}, u32[]{:S(2)}) %all-to-all-start.1) | async-done | bytes 1048608 | tf_op jit(solution)/shard_map/all_to_all | solution.py:47
  66.2 0.0 copy-start.2
  66.9 0.9 %copy-done.2 = bf16[1024,1024]{1,0:T(8,128)(2,1)S(1)} copy-done((bf16[1024,1024]{1,0:T(8,128)(2,1)S(1)}, bf16[1024,1024]{1,0:T(8,128)(2,1)}, u32[]{:S(2)}) %copy-start.2) | copy-done | bytes 2097176
  67.8 2.7 %subtract_convert_fusion = bf16[1024,1024]{1,0:T(8,128)(2,1)} fusion(bf16[1024,1024]{1,0:T(8,128)(2,1)S(1)} %copy-done.2, bf16[1024,512]{1,0:T(8,128)(2,1)S(1)} %bitcast.271, bf16[1024,512]{1,0:T(8,128)(2,1)S(1)} %constant_dynamic-update-slice_fusion), kind=kOutput, calls=%fused_computation | convolution fusion | flops 1076887552 | bytes 6291456 | tf_op jit(solution)/shard_map/dot_general | solution.py:94
  (66 shorter events, 0.3 us)
Async XLA Ops:
  0.6 5.1 %copy-start = (f32[512,512]{1,0:T(8,128)S(1)}, f32[512,512]{1,0:T(8,128)}, u32[]{:S(2)}) copy-start(f32[512,512]{1,0:T(8,128)} %param.4) | copy-start | bytes 3145732
  0.6 0.8 %collective-permute-start = (f32[128,512]{1,0:T(8,128)}, f32[128,512]{1,0:T(8,128)S(1)}, u32[]{:S(2)}, u32[]{:S(2)}) collective-permute-start(f32[128,512]{1,0:T(8,128)} %param.3), channel_id=1, source_target_pairs={{0,1},{8,9},{16,17},{24,25},{32,33},{40,41},{48,49},{56,57},{64,65... | collective-permute-start | bytes 786440 | tf_op jit(solution)/shard_map/ppermute | solution.py:28
  2.4 8.2 %collective-permute-start.2 = (f32[16,512]{1,0:T(8,128)S(1)}, f32[16,512]{1,0:T(8,128)S(1)}, u32[]{:S(2)}, u32[]{:S(2)}) collective-permute-start(f32[16,512]{1,0:T(8,128)S(1)} %get-tuple-element.6), channel_id=1, source_target_pairs={{0,8},{1,40},{8,9},{9,41},{16,10},{17,42},{24,11},{25,43},{32,12},... | collective-permute-start | bytes 98312 | tf_op jit(solution)/shard_map/ppermute | solution.py:28
  3.1 7.6 %collective-permute-start.4 = (f32[16,512]{1,0:T(8,128)S(1)}, f32[16,512]{1,0:T(8,128)S(1)}, u32[]{:S(2)}, u32[]{:S(2)}) collective-permute-start(f32[16,512]{1,0:T(8,128)S(1)} %get-tuple-element.7), channel_id=1, source_target_pairs={{0,24},{1,56},{8,25},{9,57},{16,26},{17,58},{24,27},{25,59},{32,28... | collective-permute-start | bytes 98312 | tf_op jit(solution)/shard_map/ppermute | solution.py:28
  3.8 6.9 %collective-permute-start.3 = (f32[16,512]{1,0:T(8,128)S(1)}, f32[16,512]{1,0:T(8,128)S(1)}, u32[]{:S(2)}, u32[]{:S(2)}) collective-permute-start(f32[16,512]{1,0:T(8,128)S(1)} %get-tuple-element.8), channel_id=1, source_target_pairs={{0,16},{1,48},{8,17},{9,49},{16,18},{17,50},{24,19},{25,51},{32,20... | collective-permute-start | bytes 98312 | tf_op jit(solution)/shard_map/ppermute | solution.py:28
  4.4 13.3 %collective-permute-start.1 = (f32[16,512]{1,0:T(8,128)S(1)}, f32[16,512]{1,0:T(8,128)S(1)}, u32[]{:S(2)}, u32[]{:S(2)}) collective-permute-start(f32[16,512]{1,0:T(8,128)S(1)} %get-tuple-element.9), channel_id=1, source_target_pairs={{0,0},{1,32},{8,1},{9,33},{16,2},{17,34},{24,3},{25,35},{32,4},{33... | collective-permute-start | bytes 98312 | tf_op jit(solution)/shard_map/ppermute | solution.py:28
  7.9 40.7 %copy-start.1 = (bf16[128,512]{1,0:T(8,128)(2,1)}, bf16[128,512]{1,0:T(8,128)(2,1)S(1)}, u32[]{:S(2)}) copy-start(bf16[128,512]{1,0:T(8,128)(2,1)S(1)} %convolution_convert_fusion) | copy-start | bytes 393220
  7.9 27.2 %collective-permute-start.5 = (bf16[128,512]{1,0:T(8,128)(2,1)S(1)}, bf16[128,512]{1,0:T(8,128)(2,1)S(1)}, u32[]{:S(2)}, u32[]{:S(2)}) collective-permute-start(bf16[128,512]{1,0:T(8,128)(2,1)S(1)} %convolution_convert_fusion), channel_id=1, source_target_pairs={{0,2},{1,3},{2,0},{3,1},{4,6},{5,7},{6,4},{7,5},{8,10},{9,11},{10,... | collective-permute-start | bytes 393224 | tf_op jit(solution)/shard_map/ppermute | solution.py:28
  19.4 28.1 %all-to-all-start = ((bf16[8,16,512]{2,1,0:T(8,128)(2,1)}), bf16[8,16,512]{2,1,0:T(8,128)(2,1)S(1)}, u32[]{:S(2)}, u32[]{:S(2)}) async-start(bf16[8,16,512]{2,1,0:T(8,128)(2,1)} %broadcast_in_dim.4), calls=%async_computation | async-start | bytes 262144 | tf_op jit(solution)/shard_map/all_to_all | solution.py:84
  35.1 12.3 %collective-permute-start.6 = (bf16[2,128,512]{2,1,0:T(8,128)(2,1)S(1)}, bf16[2,128,512]{2,1,0:T(8,128)(2,1)S(1)}, u32[]{:S(2)}, u32[]{:S(2)}) collective-permute-start(bf16[2,128,512]{2,1,0:T(8,128)(2,1)S(1)} %pad_maximum_fusion.1), channel_id=1, source_target_pairs={{0,4},{1,5},{2,6},{3,7},{4,0},{5,1},{6,2},{7,3},{8,12},{9,13},{10,... | collective-permute-start | bytes 786440 | tf_op jit(solution)/shard_map/ppermute | solution.py:28
  48.6 17.6 %all-to-all-start.1 = ((bf16[8,8,16,512]{3,2,1,0:T(8,128)(2,1)}), bf16[8,8,16,512]{3,2,1,0:T(8,128)(2,1)S(1)}, u32[]{:S(2)}, u32[]{:S(2)}) async-start(bf16[8,8,16,512]{3,2,1,0:T(8,128)(2,1)} %broadcast_in_dim.5), calls=%async_computation.1 | async-start | bytes 2097152 | tf_op jit(solution)/shard_map/all_to_all | solution.py:47
  52.1 3.8 %collective-permute-start.7 = (bf16[4,128,512]{2,1,0:T(8,128)(2,1)S(1)}, bf16[4,128,512]{2,1,0:T(8,128)(2,1)S(1)}, u32[]{:S(2)}, u32[]{:S(2)}) collective-permute-start(bf16[4,128,512]{2,1,0:T(8,128)(2,1)S(1)} %pad_maximum_fusion), channel_id=1, source_target_pairs={{0,1},{1,0},{2,3},{3,2},{4,5},{5,4},{6,7},{7,6},{8,9},{9,8},{10,11... | collective-permute-start | bytes 1572872 | tf_op jit(solution)/shard_map/ppermute | solution.py:28
  66.2 1.6 %copy-start.2 = (bf16[1024,1024]{1,0:T(8,128)(2,1)S(1)}, bf16[1024,1024]{1,0:T(8,128)(2,1)}, u32[]{:S(2)}) copy-start(bf16[1024,1024]{1,0:T(8,128)(2,1)} %param.5) | copy-start | bytes 6291460

commit v3 on v2

--- a/solution.py
+++ b/solution.py
@@ -13,7 +13,7 @@
 PIECE = TILE // COLS
 BLOCK = ROWS // COLS
 WIDE = 2 * TILE
-T_ORDER = [6, 7, 0, 1, 2, 3, 4, 5]
+T_ORDER = [6, 2, 0, 4, 7, 3, 1, 5]
 J_ORDER = [4, 5, 6, 7, 0, 1, 2, 3]
 APART = [[t * COLS + j for t in T_ORDER] for j in range(COLS)]
 NEAR = [[t * COLS + j for j in J_ORDER] for t in range(BLOCK)]
@@ -64,37 +64,88 @@
     return total
 
 
-def assemble(mine, other):
+def update_kernel(mine_ref, other_ref, near_ref, slab_ref, out_ref, rows_ref, old_ref, new_ref, in_sem, out_sem):
+    steps, rows, wide = old_ref.shape
+    reads = [
+        pltpu.make_async_copy(slab_ref.at[:, pl.ds(n * wide, wide)], old_ref.at[n], in_sem.at[n])
+        for n in range(steps)
+    ]
+    for read in reads:
+        read.start()
     my_col = lax.axis_index("col")
     chip, core = my_col // 2, my_col % 2
-    pair = jnp.where(core == 0, jnp.stack([mine, other], 1), jnp.stack([other, mine], 1))
-    pair = pair.reshape(2, 2, WIDE, NB)
-    pair = jnp.where(chip % 2 == 0, pair, pair[:, ::-1])
-    pair = jnp.where(chip // 2 == 0, pair, pair[::-1])
-    return pair.reshape(COLS * TILE, NB)
+    for m in range(CHIPS):
+        base = (chip ^ m) * WIDE
+        rows_ref[pl.ds(pl.multiple_of(base + core * TILE, TILE), TILE), :] = mine_ref[m]
+        rows_ref[pl.ds(pl.multiple_of(base + (1 - core) * TILE, TILE), TILE), :] = other_ref[m]
+    writes = []
+    for n in range(steps):
+        mirror = jnp.concatenate(
+            [
+                near_ref[J_ORDER.index(j), T_ORDER.index(n * (wide // TILE) + t)]
+                for t in range(wide // TILE)
+                for j in range(COLS)
+            ],
+            axis=0,
+        )
+        reads[n].wait()
+        for part in range(2):
+            for step in range(part * rows // 2, (part + 1) * rows // 2, 256):
+                here = pl.ds(step, 256)
+                product = lax.dot_general(
+                    rows_ref[here, :], mirror, (((1,), (1,)), ((), ())), preferred_element_type=jnp.float32
+                )
+                new_ref[n, here, :] = (old_ref[n, here, :].astype(jnp.float32) - product).astype(jnp.bfloat16)
+            half = pl.ds(part * rows // 2, rows // 2)
+            write = pltpu.make_async_copy(
+                new_ref.at[n, half], out_ref.at[half, pl.ds(n * wide, wide)], out_sem.at[n, part]
+            )
+            write.start()
+            writes.append(write)
+    for write in writes:
+        write.wait()
+
+
+def update(mine, other, near, slab):
+    rows, columns = slab.shape
+    whole = pl.BlockSpec(memory_space=pltpu.VMEM)
+    outside = pl.BlockSpec(memory_space=pltpu.HBM)
+    steps = columns // WIDE
+    return pl.pallas_call(
+        update_kernel,
+        in_specs=[whole, whole, whole, outside],
+        out_specs=outside,
+        out_shape=jax.ShapeDtypeStruct(slab.shape, slab.dtype),
+        scratch_shapes=[
+            pltpu.VMEM((rows, NB), jnp.bfloat16),
+            pltpu.VMEM((steps, rows, WIDE), jnp.bfloat16),
+            pltpu.VMEM((steps, rows, WIDE), jnp.bfloat16),
+            pltpu.SemaphoreType.DMA((steps,)),
+            pltpu.SemaphoreType.DMA((steps, 2)),
+        ],
+        compiler_params=pltpu.CompilerParams(vmem_limit_bytes=51 * 1024 * 1024),
+        cost_estimate=pl.CostEstimate(
+            flops=2 * rows * columns * NB, bytes_accessed=6 * rows * columns, transcendentals=0
+        ),
+    )(mine, other, near, slab)
 
 
 def shards(panel, inverse_factor, slab):
     own_factor = solve_panel(panel, inverse_factor)
-    one = permute(own_factor, everywhere(lambda r, c: (r, c ^ 2)))
     leading = scatter(panel)
     piece = solve_panel(leading, inverse_factor)
     copies = jnp.broadcast_to(piece[None], (BLOCK, PIECE, NB))
-    two = jnp.stack([own_factor, one])
+    copies, own_rows = lax.optimization_barrier((copies, own_factor))
     far = lax.all_to_all(copies, "row", 0, 0, axis_index_groups=APART, tiled=True)
-    four = jnp.concatenate([two, permute(two, everywhere(lambda r, c: (r, c ^ 4)))])
-    far, four = lax.optimization_barrier((far, four))
+    one = permute(own_rows, everywhere(lambda r, c: (r, c ^ 2)))
+    three = permute(own_rows, everywhere(lambda r, c: (r, c ^ 6)))
+    far, one, three, own_late = lax.optimization_barrier((far, one, three, own_rows))
     near = spread(far, "row", NEAR, COLS)
+    two = permute(own_late, everywhere(lambda r, c: (r, c ^ 4)))
+    four = jnp.stack([own_late, one, two, three])
     other = permute(four, everywhere(lambda r, c: (r, c ^ 1)))
-    factor_rows = assemble(four, other)
-    near = near.reshape(COLS, BLOCK, PIECE, NB)
-    mirror = jnp.concatenate(
-        [near[J_ORDER.index(j), T_ORDER.index(t)] for t in range(BLOCK) for j in range(COLS)]
-    )
-    product = lax.dot_general(
-        factor_rows, mirror, (((1,), (1,)), ((), ())), preferred_element_type=jnp.float32
-    )
-    return own_factor, (slab.astype(jnp.float32) - product).astype(jnp.bfloat16)
+    updated_slab = update(four, other, near.reshape(COLS, BLOCK, PIECE, NB), slab)
+    return own_factor, updated_slab
 
 
 def solution(mesh):

time: 71.3 us -> 68.9 us (0.966)
  Pallas kernels: 0 us -> 3.78 us
  matrix products: 5.75 us -> 3.09 us
  waiting for transfers between devices: 27.5 us -> 25.3 us
  local copies, waits for them, and re-layouts: 2.98 us -> 1.81 us
  starting transfers between devices: 31.3 us -> 32.2 us
    all_to_all x1, waiting for transfers between devices: 9.57 us -> 1.09 us  [spread(): lax.all_to_all(copies, axis, 0, 0, axis_index_groups=groups, tiled=True)]
    ppermute x8 -> x9, waiting for transfers between devices: 17.9 us -> 23.5 us  [permute(): lax.ppermute(value, MESH_AXES, [(device(*a), device(*b)) for a, b in pairs])]
    pallas_call x0 -> x1, Pallas kernels: none -> 3.78 us  [update(): pl.pallas_call(update_kernel, in_specs=[whole, whole, whole, outside], ou...]
    dot_general x1 -> x0, matrix products: 2.66 us -> none  [shards(): lax.dot_general(factor_rows, mirror, (((1,), (1,)), ((), ())), preferred_...]
    unnamed x69 -> x4, local copies, waits for them, and re-layouts: 1.12 us -> 0.02 us
    all_to_all x1, starting transfers between devices: 3.51 us -> 4.46 us  [spread(): lax.all_to_all(copies, axis, 0, 0, axis_index_groups=groups, tiled=True)]
    all_to_all x1, waiting for transfers between devices: 0.01 us -> 0.72 us  [shards(): lax.all_to_all(copies, 'row', 0, 0, axis_index_groups=APART, tiled=True)]
    ppermute x8 -> x9, starting transfers between devices: 12.1 us -> 12.1 us  [permute(): lax.ppermute(value, MESH_AXES, [(device(*a), device(*b)) for a, b in pairs])]
  transfers between devices with their start and end apart: 10 -> 11, of which waited for: 4 -> 7; matrix products, arithmetic and copies ran while one was open for 6% -> 3% of each run, Pallas kernels for 0% -> 0%
where the time goes in v3:
time: 68.9 us; the launch traced here: 68 us
  starting transfers between devices  32.2 us (47%)
  waiting for transfers between devices  25.3 us (37%)
  Pallas kernels  3.78 us (5%)
  matrix products  3.09 us (4%)
  local copies, waits for them, and re-layouts  1.81 us (3%)
  other arithmetic  0.99 us (1%)
  between operations  0.79 us (1%)
    ppermute x9, waiting for transfers between devices, permute(): lax.ppermute(value, MESH_AXES, [(device(*a), device(*b)) for a, b in pairs])  23.5 us
    all_to_all x1, starting transfers between devices, shards(): lax.all_to_all(copies, 'row', 0, 0, axis_index_groups=APART, tiled=True)  15.6 us
    ppermute x9, starting transfers between devices, permute(): lax.ppermute(value, MESH_AXES, [(device(*a), device(*b)) for a, b in pairs])  12.1 us
    all_to_all x1, starting transfers between devices, spread(): lax.all_to_all(copies, axis, 0, 0, axis_index_groups=groups, tiled=True)  4.46 us
    pallas_call x1, Pallas kernels, update(): pl.pallas_call(update_kernel, in_specs=[whole, whole, whole, outside], ou...  3.78 us
    dot_general x2, matrix products, solve_panel(): lax.dot_general(rows, inverse_factor, (((1,), (1,)), ((), ())), precision...  3.09 us
  transfers between devices with their start and end apart: 11, of which 7 were waited for; matrix products, arithmetic and copies ran while one was open for 3% of the time, Pallas kernels for 0%

profile of v3, /device:TPU:6, one launch (start us, length us, event | category | flops | bytes accessed | tf_op | source)
XLA Modules:
  0.0 68.0 jit_solution(9373765403013275003)
XLA Ops:
  0.6 0.0 copy-start
  0.6 0.8 %collective-permute-start = (f32[128,512]{1,0:T(8,128)}, f32[128,512]{1,0:T(8,128)S(1)}, u32[]{:S(2)}, u32[]{:S(2)}) collective-permute-start(f32[128,512]{1,0:T(8,128)} %param.3), channel_id=1, source_target_pairs={{0,1},{8,9},{16,17},{24,25},{32,33},{40,41},{48,49},{56,57},{64,65... | collective-permute-start | bytes 786440 | tf_op jit(solution)/shard_map/ppermute | solution.py:28
  1.5 0.0 collective-permute-done
  1.5 0.9 %slice_select_fusion = f32[64,512]{1,0:T(8,128)S(1)} fusion(f32[128,512]{1,0:T(8,128)S(1)} %collective-permute-done, f32[128,512]{1,0:T(8,128)} %param.3, pred[]{:T(512)S(6)} %eq.3), kind=kLoop, calls=%fused_computation.3 | loop fusion | flops 32768 | bytes 393217 | tf_op jit(solution)/shard_map/jit(_where)/select_n | solution.py:53
  2.4 0.7 collective-permute-start.2
  3.1 0.7 collective-permute-start.4
  3.8 0.7 collective-permute-start.3
  4.4 1.3 %collective-permute-start.1 = (f32[16,512]{1,0:T(8,128)S(1)}, f32[16,512]{1,0:T(8,128)S(1)}, u32[]{:S(2)}, u32[]{:S(2)}) collective-permute-start(f32[16,512]{1,0:T(8,128)S(1)} %get-tuple-element.17), channel_id=1, source_target_pairs={{0,0},{1,32},{8,1},{9,33},{16,2},{17,34},{24,3},{25,35},{32,4},{33... | collective-permute-start | bytes 98312 | tf_op jit(solution)/shard_map/ppermute | solution.py:28
  5.7 0.0 copy-done
  5.7 2.1 %convolution_convert_fusion = bf16[128,512]{1,0:T(8,128)(2,1)S(1)} fusion(f32[128,512]{1,0:T(8,128)} %param.3, f32[512,512]{1,0:T(8,128)S(1)} %copy-done), kind=kOutput, calls=%fused_computation | convolution fusion | flops 402718720 | bytes 1441792 | tf_op jit(solution)/shard_map/dot_general | solution.py:36
  7.9 0.0 copy-start.1
  7.9 0.0 collective-permute-done.2
  7.9 0.0 collective-permute-done.4
  7.9 0.0 collective-permute-done.3
  7.9 9.9 %collective-permute-done.1 = f32[16,512]{1,0:T(8,128)S(1)} collective-permute-done((f32[16,512]{1,0:T(8,128)S(1)}, f32[16,512]{1,0:T(8,128)S(1)}, u32[]{:S(2)}, u32[]{:S(2)}) %collective-permute-start.1) | collective-permute-done | bytes 32800 | tf_op jit(solution)/shard_map/ppermute | solution.py:28
  17.8 1.0 %convolution_convert_fusion.1 = bf16[16,512]{1,0:T(8,128)(2,1)S(1)} fusion(f32[512,512]{1,0:T(8,128)S(1)} %copy-done, f32[16,512]{1,0:T(8,128)S(1)} %collective-permute-done.4, f32[16,512]{1,0:T(8,128)S(1)} %collective-permute-done.3, f32[16,512]{1,0:T(8,128)S(1)} %collective-permute-done.1, f32[16,512]{1,0:T(8,128)S(1)} %collective-permute-done.2), kind=kOutput, calls=%fused_computation.1 | convolution fusion | flops 50364416 | bytes 1196032 | tf_op jit(solution)/shard_map/dot_general | solution.py:36
  18.7 0.7 %broadcast_in_dim.4 = bf16[8,16,512]{2,1,0:T(8,128)(2,1)} broadcast(bf16[16,512]{1,0:T(8,128)(2,1)S(1)} %convolution_convert_fusion.1), dimensions={1,2} | broadcast | bytes 147456 | tf_op jit(solution)/shard_map/broadcast_in_dim | solution.py:137
  19.4 15.6 %all-to-all-start = ((bf16[8,16,512]{2,1,0:T(8,128)(2,1)}), bf16[8,16,512]{2,1,0:T(8,128)(2,1)S(1)}, u32[]{:S(2)}, u32[]{:S(2)}) async-start(bf16[8,16,512]{2,1,0:T(8,128)(2,1)} %broadcast_in_dim.4), calls=%async_computation | async-start | bytes 262144 | tf_op jit(solution)/shard_map/all_to_all | solution.py:139
  35.1 1.9 %collective-permute-start.6 = (bf16[128,512]{1,0:T(8,128)(2,1)S(1)}, bf16[128,512]{1,0:T(8,128)(2,1)S(1)}, u32[]{:S(2)}, u32[]{:S(2)}) collective-permute-start(bf16[128,512]{1,0:T(8,128)(2,1)S(1)} %convolution_convert_fusion), channel_id=1, source_target_pairs={{0,6},{1,7},{2,4},{3,5},{4,2},{5,3},{6,0},{7,1},{8,14},{9,15},{10,... | collective-permute-start | bytes 393224 | tf_op jit(solution)/shard_map/ppermute | solution.py:28
  37.0 1.9 %collective-permute-start.5 = (bf16[128,512]{1,0:T(8,128)(2,1)S(1)}, bf16[128,512]{1,0:T(8,128)(2,1)S(1)}, u32[]{:S(2)}, u32[]{:S(2)}) collective-permute-start(bf16[128,512]{1,0:T(8,128)(2,1)S(1)} %convolution_convert_fusion), channel_id=1, source_target_pairs={{0,2},{1,3},{2,0},{3,1},{4,6},{5,7},{6,4},{7,5},{8,10},{9,11},{10,... | collective-permute-start | bytes 393224 | tf_op jit(solution)/shard_map/ppermute | solution.py:28
  38.9 4.2 %collective-permute-done.6 = bf16[128,512]{1,0:T(8,128)(2,1)S(1)} collective-permute-done((bf16[128,512]{1,0:T(8,128)(2,1)S(1)}, bf16[128,512]{1,0:T(8,128)(2,1)S(1)}, u32[]{:S(2)}, u32[]{:S(2)}) %collective-permute-start.6) | collective-permute-done | bytes 131104 | tf_op jit(solution)/shard_map/ppermute | solution.py:28
  43.1 1.4 %collective-permute-done.5 = bf16[128,512]{1,0:T(8,128)(2,1)S(1)} collective-permute-done((bf16[128,512]{1,0:T(8,128)(2,1)S(1)}, bf16[128,512]{1,0:T(8,128)(2,1)S(1)}, u32[]{:S(2)}, u32[]{:S(2)}) %collective-permute-start.5) | collective-permute-done | bytes 131104 | tf_op jit(solution)/shard_map/ppermute | solution.py:28
  44.6 0.7 %all-to-all-done = bf16[8,16,512]{2,1,0:T(8,128)(2,1)S(1)} async-done(((bf16[8,16,512]{2,1,0:T(8,128)(2,1)}), bf16[8,16,512]{2,1,0:T(8,128)(2,1)S(1)}, u32[]{:S(2)}, u32[]{:S(2)}) %all-to-all-start) | async-done | bytes 131104 | tf_op jit(solution)/shard_map/all_to_all | solution.py:139
  45.3 1.1 %broadcast_in_dim.5 = bf16[8,8,16,512]{3,2,1,0:T(8,128)(2,1)} broadcast(bf16[8,16,512]{2,1,0:T(8,128)(2,1)S(1)} %all-to-all-done), dimensions={1,2,3} | broadcast | bytes 1179648 | tf_op jit(solution)/shard_map/broadcast_in_dim | solution.py:46
  46.4 4.5 %all-to-all-start.1 = ((bf16[8,8,16,512]{3,2,1,0:T(8,128)(2,1)}), bf16[8,8,16,512]{3,2,1,0:T(8,128)(2,1)S(1)}, u32[]{:S(2)}, u32[]{:S(2)}) async-start(bf16[8,8,16,512]{3,2,1,0:T(8,128)(2,1)} %broadcast_in_dim.5), calls=%async_computation.1 | async-start | bytes 2097152 | tf_op jit(solution)/shard_map/all_to_all | solution.py:47
  50.9 2.2 %collective-permute-start.7 = (bf16[128,512]{1,0:T(8,128)(2,1)S(1)}, bf16[128,512]{1,0:T(8,128)(2,1)S(1)}, u32[]{:S(2)}, u32[]{:S(2)}) collective-permute-start(bf16[128,512]{1,0:T(8,128)(2,1)S(1)} %convolution_convert_fusion), channel_id=1, source_target_pairs={{0,4},{1,5},{2,6},{3,7},{4,0},{5,1},{6,2},{7,3},{8,12},{9,13},{10,... | collective-permute-start | bytes 393224 | tf_op jit(solution)/shard_map/ppermute | solution.py:28
  53.1 6.2 %collective-permute-done.7 = bf16[128,512]{1,0:T(8,128)(2,1)S(1)} collective-permute-done((bf16[128,512]{1,0:T(8,128)(2,1)S(1)}, bf16[128,512]{1,0:T(8,128)(2,1)S(1)}, u32[]{:S(2)}, u32[]{:S(2)}) %collective-permute-start.7) | collective-permute-done | bytes 131104 | tf_op jit(solution)/shard_map/ppermute | solution.py:28
  59.2 0.0 copy-done.1
  59.2 0.1 pad_maximum_fusion.mine_ref
  59.3 1.9 %collective-permute-start.8 = (bf16[4,128,512]{2,1,0:T(8,128)(2,1)S(1)}, bf16[4,128,512]{2,1,0:T(8,128)(2,1)S(1)}, u32[]{:S(2)}, u32[]{:S(2)}) collective-permute-start(bf16[4,128,512]{2,1,0:T(8,128)(2,1)S(1)} %pad_maximum_fusion.mine_ref), channel_id=1, source_target_pairs={{0,1},{1,0},{2,3},{3,2},{4,5},{5,4},{6,7},{7,6},{8,9},{9,8},{10,11... | collective-permute-start | bytes 1572872 | tf_op jit(solution)/shard_map/ppermute | solution.py:28
  61.2 1.9 %collective-permute-done.8.other_ref = bf16[4,128,512]{2,1,0:T(8,128)(2,1)S(1)} collective-permute-done((bf16[4,128,512]{2,1,0:T(8,128)(2,1)S(1)}, bf16[4,128,512]{2,1,0:T(8,128)(2,1)S(1)}, u32[]{:S(2)}, u32[]{:S(2)}) %collective-permute-start.8) | collective-permute-done | bytes 524320 | tf_op jit(solution)/shard_map/ppermute | solution.py:28
  63.1 1.1 %all-to-all-done.1.near_ref = bf16[8,8,16,512]{3,2,1,0:T(8,128)(2,1)S(1)} async-done(((bf16[8,8,16,512]{3,2,1,0:T(8,128)(2,1)}), bf16[8,8,16,512]{3,2,1,0:T(8,128)(2,1)S(1)}, u32[]{:S(2)}, u32[]{:S(2)}) %all-to-all-start.1) | async-done | bytes 1048608 | tf_op jit(solution)/shard_map/all_to_all | solution.py:47
  64.2 3.8 %shard_map.50 = bf16[1024,1024]{1,0:T(8,128)(2,1)} custom-call(bf16[4,128,512]{2,1,0:T(8,128)(2,1)S(1)} %pad_maximum_fusion.mine_ref, bf16[4,128,512]{2,1,0:T(8,128)(2,1)S(1)} %collective-permute-done.8.other_ref, bf16[8,8,16,512]{3,2,1,0:T(8,128)(2,1)S(1)} %all-to-all-done.1.near_ref, bf16[1024,1024]{1,0:T(8,128)(2,1)} %slab_ref.1), custom_call_target="tpu_custom_call" | custom-call | flops 1073741824 | bytes 6291456 | tf_op jit(solution)/shard_map/pallas_call | solution.py:114
  (1 shorter events, 0.0 us)
Async XLA Ops:
  0.6 5.1 %copy-start = (f32[512,512]{1,0:T(8,128)S(1)}, f32[512,512]{1,0:T(8,128)}, u32[]{:S(2)}) copy-start(f32[512,512]{1,0:T(8,128)} %param.4) | copy-start | bytes 3145732
  0.6 0.8 %collective-permute-start = (f32[128,512]{1,0:T(8,128)}, f32[128,512]{1,0:T(8,128)S(1)}, u32[]{:S(2)}, u32[]{:S(2)}) collective-permute-start(f32[128,512]{1,0:T(8,128)} %param.3), channel_id=1, source_target_pairs={{0,1},{8,9},{16,17},{24,25},{32,33},{40,41},{48,49},{56,57},{64,65... | collective-permute-start | bytes 786440 | tf_op jit(solution)/shard_map/ppermute | solution.py:28
  2.4 5.5 %collective-permute-start.2 = (f32[16,512]{1,0:T(8,128)S(1)}, f32[16,512]{1,0:T(8,128)S(1)}, u32[]{:S(2)}, u32[]{:S(2)}) collective-permute-start(f32[16,512]{1,0:T(8,128)S(1)} %get-tuple-element.14), channel_id=1, source_target_pairs={{0,8},{1,40},{8,9},{9,41},{16,10},{17,42},{24,11},{25,43},{32,12},... | collective-permute-start | bytes 98312 | tf_op jit(solution)/shard_map/ppermute | solution.py:28
  3.1 4.8 %collective-permute-start.4 = (f32[16,512]{1,0:T(8,128)S(1)}, f32[16,512]{1,0:T(8,128)S(1)}, u32[]{:S(2)}, u32[]{:S(2)}) collective-permute-start(f32[16,512]{1,0:T(8,128)S(1)} %get-tuple-element.15), channel_id=1, source_target_pairs={{0,24},{1,56},{8,25},{9,57},{16,26},{17,58},{24,27},{25,59},{32,28... | collective-permute-start | bytes 98312 | tf_op jit(solution)/shard_map/ppermute | solution.py:28
  3.8 4.2 %collective-permute-start.3 = (f32[16,512]{1,0:T(8,128)S(1)}, f32[16,512]{1,0:T(8,128)S(1)}, u32[]{:S(2)}, u32[]{:S(2)}) collective-permute-start(f32[16,512]{1,0:T(8,128)S(1)} %get-tuple-element.16), channel_id=1, source_target_pairs={{0,16},{1,48},{8,17},{9,49},{16,18},{17,50},{24,19},{25,51},{32,20... | collective-permute-start | bytes 98312 | tf_op jit(solution)/shard_map/ppermute | solution.py:28
  4.4 13.3 %collective-permute-start.1 = (f32[16,512]{1,0:T(8,128)S(1)}, f32[16,512]{1,0:T(8,128)S(1)}, u32[]{:S(2)}, u32[]{:S(2)}) collective-permute-start(f32[16,512]{1,0:T(8,128)S(1)} %get-tuple-element.17), channel_id=1, source_target_pairs={{0,0},{1,32},{8,1},{9,33},{16,2},{17,34},{24,3},{25,35},{32,4},{33... | collective-permute-start | bytes 98312 | tf_op jit(solution)/shard_map/ppermute | solution.py:28
  7.9 51.3 %copy-start.1 = (bf16[128,512]{1,0:T(8,128)(2,1)}, bf16[128,512]{1,0:T(8,128)(2,1)S(1)}, u32[]{:S(2)}) copy-start(bf16[128,512]{1,0:T(8,128)(2,1)S(1)} %convolution_convert_fusion) | copy-start | bytes 393220
  19.4 25.9 %all-to-all-start = ((bf16[8,16,512]{2,1,0:T(8,128)(2,1)}), bf16[8,16,512]{2,1,0:T(8,128)(2,1)S(1)}, u32[]{:S(2)}, u32[]{:S(2)}) async-start(bf16[8,16,512]{2,1,0:T(8,128)(2,1)} %broadcast_in_dim.4), calls=%async_computation | async-start | bytes 262144 | tf_op jit(solution)/shard_map/all_to_all | solution.py:139
  35.1 8.1 %collective-permute-start.6 = (bf16[128,512]{1,0:T(8,128)(2,1)S(1)}, bf16[128,512]{1,0:T(8,128)(2,1)S(1)}, u32[]{:S(2)}, u32[]{:S(2)}) collective-permute-start(bf16[128,512]{1,0:T(8,128)(2,1)S(1)} %convolution_convert_fusion), channel_id=1, source_target_pairs={{0,6},{1,7},{2,4},{3,5},{4,2},{5,3},{6,0},{7,1},{8,14},{9,15},{10,... | collective-permute-start | bytes 393224 | tf_op jit(solution)/shard_map/ppermute | solution.py:28
  37.0 7.6 %collective-permute-start.5 = (bf16[128,512]{1,0:T(8,128)(2,1)S(1)}, bf16[128,512]{1,0:T(8,128)(2,1)S(1)}, u32[]{:S(2)}, u32[]{:S(2)}) collective-permute-start(bf16[128,512]{1,0:T(8,128)(2,1)S(1)} %convolution_convert_fusion), channel_id=1, source_target_pairs={{0,2},{1,3},{2,0},{3,1},{4,6},{5,7},{6,4},{7,5},{8,10},{9,11},{10,... | collective-permute-start | bytes 393224 | tf_op jit(solution)/shard_map/ppermute | solution.py:28
  46.4 17.8 %all-to-all-start.1 = ((bf16[8,8,16,512]{3,2,1,0:T(8,128)(2,1)}), bf16[8,8,16,512]{3,2,1,0:T(8,128)(2,1)S(1)}, u32[]{:S(2)}, u32[]{:S(2)}) async-start(bf16[8,8,16,512]{3,2,1,0:T(8,128)(2,1)} %broadcast_in_dim.5), calls=%async_computation.1 | async-start | bytes 2097152 | tf_op jit(solution)/shard_map/all_to_all | solution.py:47
  50.9 8.4 %collective-permute-start.7 = (bf16[128,512]{1,0:T(8,128)(2,1)S(1)}, bf16[128,512]{1,0:T(8,128)(2,1)S(1)}, u32[]{:S(2)}, u32[]{:S(2)}) collective-permute-start(bf16[128,512]{1,0:T(8,128)(2,1)S(1)} %convolution_convert_fusion), channel_id=1, source_target_pairs={{0,4},{1,5},{2,6},{3,7},{4,0},{5,1},{6,2},{7,3},{8,12},{9,13},{10,... | collective-permute-start | bytes 393224 | tf_op jit(solution)/shard_map/ppermute | solution.py:28
  59.3 3.8 %collective-permute-start.8 = (bf16[4,128,512]{2,1,0:T(8,128)(2,1)S(1)}, bf16[4,128,512]{2,1,0:T(8,128)(2,1)S(1)}, u32[]{:S(2)}, u32[]{:S(2)}) collective-permute-start(bf16[4,128,512]{2,1,0:T(8,128)(2,1)S(1)} %pad_maximum_fusion.mine_ref), channel_id=1, source_target_pairs={{0,1},{1,0},{2,3},{3,2},{4,5},{5,4},{6,7},{7,6},{8,9},{9,8},{10,11... | collective-permute-start | bytes 1572872 | tf_op jit(solution)/shard_map/ppermute | solution.py:28

commit v4 on v3

--- a/solution.py
+++ b/solution.py
@@ -110,7 +110,7 @@
     rows, columns = slab.shape
     whole = pl.BlockSpec(memory_space=pltpu.VMEM)
     outside = pl.BlockSpec(memory_space=pltpu.HBM)
-    steps = columns // WIDE
+    steps = columns // (2 * WIDE)
     return pl.pallas_call(
         update_kernel,
         in_specs=[whole, whole, whole, outside],
@@ -118,8 +118,8 @@
         out_shape=jax.ShapeDtypeStruct(slab.shape, slab.dtype),
         scratch_shapes=[
             pltpu.VMEM((rows, NB), jnp.bfloat16),
-            pltpu.VMEM((steps, rows, WIDE), jnp.bfloat16),
-            pltpu.VMEM((steps, rows, WIDE), jnp.bfloat16),
+            pltpu.VMEM((steps, rows, 2 * WIDE), jnp.bfloat16),
+            pltpu.VMEM((steps, rows, 2 * WIDE), jnp.bfloat16),
             pltpu.SemaphoreType.DMA((steps,)),
             pltpu.SemaphoreType.DMA((steps, 2)),
         ],
@@ -138,10 +138,10 @@
     copies, own_rows = lax.optimization_barrier((copies, own_factor))
     far = lax.all_to_all(copies, "row", 0, 0, axis_index_groups=APART, tiled=True)
     one = permute(own_rows, everywhere(lambda r, c: (r, c ^ 2)))
-    three = permute(own_rows, everywhere(lambda r, c: (r, c ^ 6)))
-    far, one, three, own_late = lax.optimization_barrier((far, one, three, own_rows))
+    two = permute(own_rows, everywhere(lambda r, c: (r, c ^ 4)))
+    far, one, two, own_late = lax.optimization_barrier((far, one, two, own_rows))
     near = spread(far, "row", NEAR, COLS)
-    two = permute(own_late, everywhere(lambda r, c: (r, c ^ 4)))
+    three = permute(own_late, everywhere(lambda r, c: (r, c ^ 6)))
     four = jnp.stack([own_late, one, two, three])
     other = permute(four, everywhere(lambda r, c: (r, c ^ 1)))
     updated_slab = update(four, other, near.reshape(COLS, BLOCK, PIECE, NB), slab)

time: 68.9 us -> 68.8 us (level)
    ppermute x9, starting transfers between devices: 12.1 us -> 12.8 us  [permute(): lax.ppermute(value, MESH_AXES, [(device(*a), device(*b)) for a, b in pairs])]
where the time goes in v4:
time: 68.8 us; the launch traced here: 67.6 us
  starting transfers between devices  32.4 us (47%)
  waiting for transfers between devices  24.8 us (36%)
  Pallas kernels  3.62 us (5%)
  matrix products  3.09 us (4%)
  local copies, waits for them, and re-layouts  1.81 us (3%)
  other arithmetic  0.99 us (1%)
  between operations  0.79 us (1%)
    ppermute x9, waiting for transfers between devices, permute(): lax.ppermute(value, MESH_AXES, [(device(*a), device(*b)) for a, b in pairs])  23 us
    all_to_all x1, starting transfers between devices, shards(): lax.all_to_all(copies, 'row', 0, 0, axis_index_groups=APART, tiled=True)  15.6 us
    ppermute x9, starting transfers between devices, permute(): lax.ppermute(value, MESH_AXES, [(device(*a), device(*b)) for a, b in pairs])  12.8 us
    all_to_all x1, starting transfers between devices, spread(): lax.all_to_all(copies, axis, 0, 0, axis_index_groups=groups, tiled=True)  3.96 us
    pallas_call x1, Pallas kernels, update(): pl.pallas_call(update_kernel, in_specs=[whole, whole, whole, outside], ou...  3.62 us
    dot_general x2, matrix products, solve_panel(): lax.dot_general(rows, inverse_factor, (((1,), (1,)), ((), ())), precision...  3.09 us
    all_to_all x1, waiting for transfers between devices, spread(): lax.all_to_all(copies, axis, 0, 0, axis_index_groups=groups, tiled=True)  1.64 us
  transfers between devices with their start and end apart: 11, of which 7 were waited for; matrix products, arithmetic and copies ran while one was open for 3% of the time, Pallas kernels for 0%

profile of v4, /device:TPU:6, one launch (start us, length us, event | category | flops | bytes accessed | tf_op | source)
XLA Modules:
  0.0 67.6 jit_solution(3369969150998059415)
XLA Ops:
  0.6 0.0 copy-start
  0.6 0.8 %collective-permute-start = (f32[128,512]{1,0:T(8,128)}, f32[128,512]{1,0:T(8,128)S(1)}, u32[]{:S(2)}, u32[]{:S(2)}) collective-permute-start(f32[128,512]{1,0:T(8,128)} %param.3), channel_id=1, source_target_pairs={{0,1},{8,9},{16,17},{24,25},{32,33},{40,41},{48,49},{56,57},{64,65... | collective-permute-start | bytes 786440 | tf_op jit(solution)/shard_map/ppermute | solution.py:28
  1.5 0.0 collective-permute-done
  1.5 0.9 %slice_select_fusion = f32[64,512]{1,0:T(8,128)S(1)} fusion(f32[128,512]{1,0:T(8,128)S(1)} %collective-permute-done, f32[128,512]{1,0:T(8,128)} %param.3, pred[]{:T(512)S(6)} %eq.3), kind=kLoop, calls=%fused_computation.3 | loop fusion | flops 32768 | bytes 393217 | tf_op jit(solution)/shard_map/jit(_where)/select_n | solution.py:53
  2.4 0.7 collective-permute-start.2
  3.1 0.7 collective-permute-start.4
  3.8 0.7 collective-permute-start.3
  4.4 1.3 %collective-permute-start.1 = (f32[16,512]{1,0:T(8,128)S(1)}, f32[16,512]{1,0:T(8,128)S(1)}, u32[]{:S(2)}, u32[]{:S(2)}) collective-permute-start(f32[16,512]{1,0:T(8,128)S(1)} %get-tuple-element.17), channel_id=1, source_target_pairs={{0,0},{1,32},{8,1},{9,33},{16,2},{17,34},{24,3},{25,35},{32,4},{33... | collective-permute-start | bytes 98312 | tf_op jit(solution)/shard_map/ppermute | solution.py:28
  5.7 0.0 copy-done
  5.7 2.1 %convolution_convert_fusion = bf16[128,512]{1,0:T(8,128)(2,1)S(1)} fusion(f32[128,512]{1,0:T(8,128)} %param.3, f32[512,512]{1,0:T(8,128)S(1)} %copy-done), kind=kOutput, calls=%fused_computation | convolution fusion | flops 402718720 | bytes 1441792 | tf_op jit(solution)/shard_map/dot_general | solution.py:36
  7.9 0.0 copy-start.1
  7.9 0.0 collective-permute-done.2
  7.9 0.0 collective-permute-done.4
  7.9 0.0 collective-permute-done.3
  7.9 9.9 %collective-permute-done.1 = f32[16,512]{1,0:T(8,128)S(1)} collective-permute-done((f32[16,512]{1,0:T(8,128)S(1)}, f32[16,512]{1,0:T(8,128)S(1)}, u32[]{:S(2)}, u32[]{:S(2)}) %collective-permute-start.1) | collective-permute-done | bytes 32800 | tf_op jit(solution)/shard_map/ppermute | solution.py:28
  17.8 1.0 %convolution_convert_fusion.1 = bf16[16,512]{1,0:T(8,128)(2,1)S(1)} fusion(f32[512,512]{1,0:T(8,128)S(1)} %copy-done, f32[16,512]{1,0:T(8,128)S(1)} %collective-permute-done.4, f32[16,512]{1,0:T(8,128)S(1)} %collective-permute-done.3, f32[16,512]{1,0:T(8,128)S(1)} %collective-permute-done.1, f32[16,512]{1,0:T(8,128)S(1)} %collective-permute-done.2), kind=kOutput, calls=%fused_computation.1 | convolution fusion | flops 50364416 | bytes 1196032 | tf_op jit(solution)/shard_map/dot_general | solution.py:36
  18.7 0.7 %broadcast_in_dim.4 = bf16[8,16,512]{2,1,0:T(8,128)(2,1)} broadcast(bf16[16,512]{1,0:T(8,128)(2,1)S(1)} %convolution_convert_fusion.1), dimensions={1,2} | broadcast | bytes 147456 | tf_op jit(solution)/shard_map/broadcast_in_dim | solution.py:137
  19.4 15.6 %all-to-all-start = ((bf16[8,16,512]{2,1,0:T(8,128)(2,1)}), bf16[8,16,512]{2,1,0:T(8,128)(2,1)S(1)}, u32[]{:S(2)}, u32[]{:S(2)}) async-start(bf16[8,16,512]{2,1,0:T(8,128)(2,1)} %broadcast_in_dim.4), calls=%async_computation | async-start | bytes 262144 | tf_op jit(solution)/shard_map/all_to_all | solution.py:139
  35.1 1.9 %collective-permute-start.6 = (bf16[128,512]{1,0:T(8,128)(2,1)S(1)}, bf16[128,512]{1,0:T(8,128)(2,1)S(1)}, u32[]{:S(2)}, u32[]{:S(2)}) collective-permute-start(bf16[128,512]{1,0:T(8,128)(2,1)S(1)} %convolution_convert_fusion), channel_id=1, source_target_pairs={{0,4},{1,5},{2,6},{3,7},{4,0},{5,1},{6,2},{7,3},{8,12},{9,13},{10,... | collective-permute-start | bytes 393224 | tf_op jit(solution)/shard_map/ppermute | solution.py:28
  37.0 1.9 %collective-permute-start.5 = (bf16[128,512]{1,0:T(8,128)(2,1)S(1)}, bf16[128,512]{1,0:T(8,128)(2,1)S(1)}, u32[]{:S(2)}, u32[]{:S(2)}) collective-permute-start(bf16[128,512]{1,0:T(8,128)(2,1)S(1)} %convolution_convert_fusion), channel_id=1, source_target_pairs={{0,2},{1,3},{2,0},{3,1},{4,6},{5,7},{6,4},{7,5},{8,10},{9,11},{10,... | collective-permute-start | bytes 393224 | tf_op jit(solution)/shard_map/ppermute | solution.py:28
  38.9 5.0 %collective-permute-done.6 = bf16[128,512]{1,0:T(8,128)(2,1)S(1)} collective-permute-done((bf16[128,512]{1,0:T(8,128)(2,1)S(1)}, bf16[128,512]{1,0:T(8,128)(2,1)S(1)}, u32[]{:S(2)}, u32[]{:S(2)}) %collective-permute-start.6) | collective-permute-done | bytes 131104 | tf_op jit(solution)/shard_map/ppermute | solution.py:28
  44.0 1.1 %collective-permute-done.5 = bf16[128,512]{1,0:T(8,128)(2,1)S(1)} collective-permute-done((bf16[128,512]{1,0:T(8,128)(2,1)S(1)}, bf16[128,512]{1,0:T(8,128)(2,1)S(1)}, u32[]{:S(2)}, u32[]{:S(2)}) %collective-permute-start.5) | collective-permute-done | bytes 131104 | tf_op jit(solution)/shard_map/ppermute | solution.py:28
  45.1 0.2 all-to-all-done
  45.3 1.1 %broadcast_in_dim.5 = bf16[8,8,16,512]{3,2,1,0:T(8,128)(2,1)} broadcast(bf16[8,16,512]{2,1,0:T(8,128)(2,1)S(1)} %all-to-all-done), dimensions={1,2,3} | broadcast | bytes 1179648 | tf_op jit(solution)/shard_map/broadcast_in_dim | solution.py:46
  46.4 4.0 %all-to-all-start.1 = ((bf16[8,8,16,512]{3,2,1,0:T(8,128)(2,1)}), bf16[8,8,16,512]{3,2,1,0:T(8,128)(2,1)S(1)}, u32[]{:S(2)}, u32[]{:S(2)}) async-start(bf16[8,8,16,512]{3,2,1,0:T(8,128)(2,1)} %broadcast_in_dim.5), calls=%async_computation.1 | async-start | bytes 2097152 | tf_op jit(solution)/shard_map/all_to_all | solution.py:47
  50.4 3.0 %collective-permute-start.7 = (bf16[128,512]{1,0:T(8,128)(2,1)S(1)}, bf16[128,512]{1,0:T(8,128)(2,1)S(1)}, u32[]{:S(2)}, u32[]{:S(2)}) collective-permute-start(bf16[128,512]{1,0:T(8,128)(2,1)S(1)} %convolution_convert_fusion), channel_id=1, source_target_pairs={{0,6},{1,7},{2,4},{3,5},{4,2},{5,3},{6,0},{7,1},{8,14},{9,15},{10,... | collective-permute-start | bytes 393224 | tf_op jit(solution)/shard_map/ppermute | solution.py:28
  53.3 5.1 %collective-permute-done.7 = bf16[128,512]{1,0:T(8,128)(2,1)S(1)} collective-permute-done((bf16[128,512]{1,0:T(8,128)(2,1)S(1)}, bf16[128,512]{1,0:T(8,128)(2,1)S(1)}, u32[]{:S(2)}, u32[]{:S(2)}) %collective-permute-start.7) | collective-permute-done | bytes 131104 | tf_op jit(solution)/shard_map/ppermute | solution.py:28
  58.4 0.0 copy-done.1
  58.4 0.1 pad_maximum_fusion.mine_ref
  58.5 1.9 %collective-permute-start.8 = (bf16[4,128,512]{2,1,0:T(8,128)(2,1)S(1)}, bf16[4,128,512]{2,1,0:T(8,128)(2,1)S(1)}, u32[]{:S(2)}, u32[]{:S(2)}) collective-permute-start(bf16[4,128,512]{2,1,0:T(8,128)(2,1)S(1)} %pad_maximum_fusion.mine_ref), channel_id=1, source_target_pairs={{0,1},{1,0},{2,3},{3,2},{4,5},{5,4},{6,7},{7,6},{8,9},{9,8},{10,11... | collective-permute-start | bytes 1572872 | tf_op jit(solution)/shard_map/ppermute | solution.py:28
  60.4 1.9 %collective-permute-done.8.other_ref = bf16[4,128,512]{2,1,0:T(8,128)(2,1)S(1)} collective-permute-done((bf16[4,128,512]{2,1,0:T(8,128)(2,1)S(1)}, bf16[4,128,512]{2,1,0:T(8,128)(2,1)S(1)}, u32[]{:S(2)}, u32[]{:S(2)}) %collective-permute-start.8) | collective-permute-done | bytes 524320 | tf_op jit(solution)/shard_map/ppermute | solution.py:28
  62.3 1.6 %all-to-all-done.1.near_ref = bf16[8,8,16,512]{3,2,1,0:T(8,128)(2,1)S(1)} async-done(((bf16[8,8,16,512]{3,2,1,0:T(8,128)(2,1)}), bf16[8,8,16,512]{3,2,1,0:T(8,128)(2,1)S(1)}, u32[]{:S(2)}, u32[]{:S(2)}) %all-to-all-start.1) | async-done | bytes 1048608 | tf_op jit(solution)/shard_map/all_to_all | solution.py:47
  63.9 3.6 %shard_map.50 = bf16[1024,1024]{1,0:T(8,128)(2,1)} custom-call(bf16[4,128,512]{2,1,0:T(8,128)(2,1)S(1)} %pad_maximum_fusion.mine_ref, bf16[4,128,512]{2,1,0:T(8,128)(2,1)S(1)} %collective-permute-done.8.other_ref, bf16[8,8,16,512]{3,2,1,0:T(8,128)(2,1)S(1)} %all-to-all-done.1.near_ref, bf16[1024,1024]{1,0:T(8,128)(2,1)} %slab_ref.1), custom_call_target="tpu_custom_call" | custom-call | flops 1073741824 | bytes 6291456 | tf_op jit(solution)/shard_map/pallas_call | solution.py:114
  (1 shorter events, 0.0 us)
Async XLA Ops:
  0.6 5.1 %copy-start = (f32[512,512]{1,0:T(8,128)S(1)}, f32[512,512]{1,0:T(8,128)}, u32[]{:S(2)}) copy-start(f32[512,512]{1,0:T(8,128)} %param.4) | copy-start | bytes 3145732
  0.6 0.8 %collective-permute-start = (f32[128,512]{1,0:T(8,128)}, f32[128,512]{1,0:T(8,128)S(1)}, u32[]{:S(2)}, u32[]{:S(2)}) collective-permute-start(f32[128,512]{1,0:T(8,128)} %param.3), channel_id=1, source_target_pairs={{0,1},{8,9},{16,17},{24,25},{32,33},{40,41},{48,49},{56,57},{64,65... | collective-permute-start | bytes 786440 | tf_op jit(solution)/shard_map/ppermute | solution.py:28
  2.4 5.5 %collective-permute-start.2 = (f32[16,512]{1,0:T(8,128)S(1)}, f32[16,512]{1,0:T(8,128)S(1)}, u32[]{:S(2)}, u32[]{:S(2)}) collective-permute-start(f32[16,512]{1,0:T(8,128)S(1)} %get-tuple-element.14), channel_id=1, source_target_pairs={{0,8},{1,40},{8,9},{9,41},{16,10},{17,42},{24,11},{25,43},{32,12},... | collective-permute-start | bytes 98312 | tf_op jit(solution)/shard_map/ppermute | solution.py:28
  3.1 4.8 %collective-permute-start.4 = (f32[16,512]{1,0:T(8,128)S(1)}, f32[16,512]{1,0:T(8,128)S(1)}, u32[]{:S(2)}, u32[]{:S(2)}) collective-permute-start(f32[16,512]{1,0:T(8,128)S(1)} %get-tuple-element.15), channel_id=1, source_target_pairs={{0,24},{1,56},{8,25},{9,57},{16,26},{17,58},{24,27},{25,59},{32,28... | collective-permute-start | bytes 98312 | tf_op jit(solution)/shard_map/ppermute | solution.py:28
  3.8 4.2 %collective-permute-start.3 = (f32[16,512]{1,0:T(8,128)S(1)}, f32[16,512]{1,0:T(8,128)S(1)}, u32[]{:S(2)}, u32[]{:S(2)}) collective-permute-start(f32[16,512]{1,0:T(8,128)S(1)} %get-tuple-element.16), channel_id=1, source_target_pairs={{0,16},{1,48},{8,17},{9,49},{16,18},{17,50},{24,19},{25,51},{32,20... | collective-permute-start | bytes 98312 | tf_op jit(solution)/shard_map/ppermute | solution.py:28
  4.4 13.3 %collective-permute-start.1 = (f32[16,512]{1,0:T(8,128)S(1)}, f32[16,512]{1,0:T(8,128)S(1)}, u32[]{:S(2)}, u32[]{:S(2)}) collective-permute-start(f32[16,512]{1,0:T(8,128)S(1)} %get-tuple-element.17), channel_id=1, source_target_pairs={{0,0},{1,32},{8,1},{9,33},{16,2},{17,34},{24,3},{25,35},{32,4},{33... | collective-permute-start | bytes 98312 | tf_op jit(solution)/shard_map/ppermute | solution.py:28
  7.9 50.5 %copy-start.1 = (bf16[128,512]{1,0:T(8,128)(2,1)}, bf16[128,512]{1,0:T(8,128)(2,1)S(1)}, u32[]{:S(2)}) copy-start(bf16[128,512]{1,0:T(8,128)(2,1)S(1)} %convolution_convert_fusion) | copy-start | bytes 393220
  19.4 25.9 %all-to-all-start = ((bf16[8,16,512]{2,1,0:T(8,128)(2,1)}), bf16[8,16,512]{2,1,0:T(8,128)(2,1)S(1)}, u32[]{:S(2)}, u32[]{:S(2)}) async-start(bf16[8,16,512]{2,1,0:T(8,128)(2,1)} %broadcast_in_dim.4), calls=%async_computation | async-start | bytes 262144 | tf_op jit(solution)/shard_map/all_to_all | solution.py:139
  35.1 8.9 %collective-permute-start.6 = (bf16[128,512]{1,0:T(8,128)(2,1)S(1)}, bf16[128,512]{1,0:T(8,128)(2,1)S(1)}, u32[]{:S(2)}, u32[]{:S(2)}) collective-permute-start(bf16[128,512]{1,0:T(8,128)(2,1)S(1)} %convolution_convert_fusion), channel_id=1, source_target_pairs={{0,4},{1,5},{2,6},{3,7},{4,0},{5,1},{6,2},{7,3},{8,12},{9,13},{10,... | collective-permute-start | bytes 393224 | tf_op jit(solution)/shard_map/ppermute | solution.py:28
  37.0 8.1 %collective-permute-start.5 = (bf16[128,512]{1,0:T(8,128)(2,1)S(1)}, bf16[128,512]{1,0:T(8,128)(2,1)S(1)}, u32[]{:S(2)}, u32[]{:S(2)}) collective-permute-start(bf16[128,512]{1,0:T(8,128)(2,1)S(1)} %convolution_convert_fusion), channel_id=1, source_target_pairs={{0,2},{1,3},{2,0},{3,1},{4,6},{5,7},{6,4},{7,5},{8,10},{9,11},{10,... | collective-permute-start | bytes 393224 | tf_op jit(solution)/shard_map/ppermute | solution.py:28
  46.4 17.5 %all-to-all-start.1 = ((bf16[8,8,16,512]{3,2,1,0:T(8,128)(2,1)}), bf16[8,8,16,512]{3,2,1,0:T(8,128)(2,1)S(1)}, u32[]{:S(2)}, u32[]{:S(2)}) async-start(bf16[8,8,16,512]{3,2,1,0:T(8,128)(2,1)} %broadcast_in_dim.5), calls=%async_computation.1 | async-start | bytes 2097152 | tf_op jit(solution)/shard_map/all_to_all | solution.py:47
  50.4 8.1 %collective-permute-start.7 = (bf16[128,512]{1,0:T(8,128)(2,1)S(1)}, bf16[128,512]{1,0:T(8,128)(2,1)S(1)}, u32[]{:S(2)}, u32[]{:S(2)}) collective-permute-start(bf16[128,512]{1,0:T(8,128)(2,1)S(1)} %convolution_convert_fusion), channel_id=1, source_target_pairs={{0,6},{1,7},{2,4},{3,5},{4,2},{5,3},{6,0},{7,1},{8,14},{9,15},{10,... | collective-permute-start | bytes 393224 | tf_op jit(solution)/shard_map/ppermute | solution.py:28
  58.5 3.8 %collective-permute-start.8 = (bf16[4,128,512]{2,1,0:T(8,128)(2,1)S(1)}, bf16[4,128,512]{2,1,0:T(8,128)(2,1)S(1)}, u32[]{:S(2)}, u32[]{:S(2)}) collective-permute-start(bf16[4,128,512]{2,1,0:T(8,128)(2,1)S(1)} %pad_maximum_fusion.mine_ref), channel_id=1, source_target_pairs={{0,1},{1,0},{2,3},{3,2},{4,5},{5,4},{6,7},{7,6},{8,9},{9,8},{10,11... | collective-permute-start | bytes 1572872 | tf_op jit(solution)/shard_map/ppermute | solution.py:28

commit v5 on v4

--- a/solution.py
+++ b/solution.py
@@ -131,11 +131,12 @@
 
 
 def shards(panel, inverse_factor, slab):
-    own_factor = solve_panel(panel, inverse_factor)
     leading = scatter(panel)
     piece = solve_panel(leading, inverse_factor)
     copies = jnp.broadcast_to(piece[None], (BLOCK, PIECE, NB))
-    copies, own_rows = lax.optimization_barrier((copies, own_factor))
+    copies, late_panel = lax.optimization_barrier((copies, panel))
+    own_factor = solve_panel(late_panel, inverse_factor)
+    own_rows = own_factor
     far = lax.all_to_all(copies, "row", 0, 0, axis_index_groups=APART, tiled=True)
     one = permute(own_rows, everywhere(lambda r, c: (r, c ^ 2)))
     two = permute(own_rows, everywhere(lambda r, c: (r, c ^ 4)))

time: 68.8 us -> 70 us (1.017)
  waiting for transfers between devices: 24.8 us -> 26.7 us
  matrix products: 3.09 us -> 2.14 us
    ppermute x9, waiting for transfers between devices: 23 us -> 24.9 us  [permute(): lax.ppermute(value, MESH_AXES, [(device(*a), device(*b)) for a, b in pairs])]
    dot_general x2, matrix products: 3.09 us -> 2.14 us  [solve_panel(): lax.dot_general(rows, inverse_factor, (((1,), (1,)), ((), ())), precision...]
  transfers between devices with their start and end apart: 11 -> 11, of which waited for: 7 -> 6; matrix products, arithmetic and copies ran while one was open for 3% -> 2% of each run, Pallas kernels for 0% -> 0%
where the time goes in v5:
time: 70 us; the launch traced here: 68.7 us
  starting transfers between devices  32.6 us (47%)
  waiting for transfers between devices  26.7 us (38%)
  Pallas kernels  3.62 us (5%)
  matrix products  2.14 us (3%)
  local copies, waits for them, and re-layouts  1.81 us (3%)
  other arithmetic  0.99 us (1%)
  between operations  0.8 us (1%)
    ppermute x9, waiting for transfers between devices, permute(): lax.ppermute(value, MESH_AXES, [(device(*a), device(*b)) for a, b in pairs])  24.9 us
    all_to_all x1, starting transfers between devices, shards(): lax.all_to_all(copies, 'row', 0, 0, axis_index_groups=APART, tiled=True)  15.6 us
    ppermute x9, starting transfers between devices, permute(): lax.ppermute(value, MESH_AXES, [(device(*a), device(*b)) for a, b in pairs])  13.4 us
    all_to_all x1, starting transfers between devices, spread(): lax.all_to_all(copies, axis, 0, 0, axis_index_groups=groups, tiled=True)  3.63 us
    pallas_call x1, Pallas kernels, update(): pl.pallas_call(update_kernel, in_specs=[whole, whole, whole, outside], ou...  3.62 us
    dot_general x2, matrix products, solve_panel(): lax.dot_general(rows, inverse_factor, (((1,), (1,)), ((), ())), precision...  2.14 us
    all_to_all x1, waiting for transfers between devices, spread(): lax.all_to_all(copies, axis, 0, 0, axis_index_groups=groups, tiled=True)  1.8 us
  transfers between devices with their start and end apart: 11, of which 6 were waited for; matrix products, arithmetic and copies ran while one was open for 2% of the time, Pallas kernels for 0%

profile of v5, /device:TPU:6, one launch (start us, length us, event | category | flops | bytes accessed | tf_op | source)
XLA Modules:
  0.0 68.7 jit_solution(4439297789679363221)
XLA Ops:
  0.6 0.0 copy-start
  0.6 0.0 copy-start.1
  0.7 0.8 %collective-permute-start = (f32[128,512]{1,0:T(8,128)}, f32[128,512]{1,0:T(8,128)S(1)}, u32[]{:S(2)}, u32[]{:S(2)}) collective-permute-start(f32[128,512]{1,0:T(8,128)} %param.3), channel_id=1, source_target_pairs={{0,1},{8,9},{16,17},{24,25},{32,33},{40,41},{48,49},{56,57},{64,65... | collective-permute-start | bytes 786440 | tf_op jit(solution)/shard_map/ppermute | solution.py:28
  1.5 0.0 collective-permute-done
  1.5 0.9 %slice_select_fusion = f32[64,512]{1,0:T(8,128)S(1)} fusion(f32[128,512]{1,0:T(8,128)S(1)} %collective-permute-done, f32[128,512]{1,0:T(8,128)} %param.3, pred[]{:T(512)S(6)} %eq.3), kind=kLoop, calls=%fused_computation.3 | loop fusion | flops 32768 | bytes 393217 | tf_op jit(solution)/shard_map/jit(_where)/select_n | solution.py:53
  2.4 0.7 collective-permute-start.2
  3.1 0.7 collective-permute-start.4
  3.8 0.7 collective-permute-start.3
  4.4 1.3 %collective-permute-start.1 = (f32[16,512]{1,0:T(8,128)S(1)}, f32[16,512]{1,0:T(8,128)S(1)}, u32[]{:S(2)}, u32[]{:S(2)}) collective-permute-start(f32[16,512]{1,0:T(8,128)S(1)} %get-tuple-element.17), channel_id=1, source_target_pairs={{0,0},{1,32},{8,1},{9,33},{16,2},{17,34},{24,3},{25,35},{32,4},{33... | collective-permute-start | bytes 98312 | tf_op jit(solution)/shard_map/ppermute | solution.py:28
  5.7 0.0 collective-permute-done.2
  5.8 0.0 collective-permute-done.4
  5.8 0.0 collective-permute-done.3
  5.8 12.0 %collective-permute-done.1 = f32[16,512]{1,0:T(8,128)S(1)} collective-permute-done((f32[16,512]{1,0:T(8,128)S(1)}, f32[16,512]{1,0:T(8,128)S(1)}, u32[]{:S(2)}, u32[]{:S(2)}) %collective-permute-start.1) | collective-permute-done | bytes 32800 | tf_op jit(solution)/shard_map/ppermute | solution.py:28
  17.8 0.0 copy-done
  17.8 1.0 %convolution_convert_fusion.1 = bf16[16,512]{1,0:T(8,128)(2,1)S(1)} fusion(f32[512,512]{1,0:T(8,128)S(1)} %copy-done, f32[16,512]{1,0:T(8,128)S(1)} %collective-permute-done.4, f32[16,512]{1,0:T(8,128)S(1)} %collective-permute-done.3, f32[16,512]{1,0:T(8,128)S(1)} %collective-permute-done.1, f32[16,512]{1,0:T(8,128)S(1)} %collective-permute-done.2), kind=kOutput, calls=%fused_computation.1 | convolution fusion | flops 50364416 | bytes 1196032 | tf_op jit(solution)/shard_map/dot_general | solution.py:36
  18.8 0.7 broadcast_in_dim.4
  19.4 15.6 %all-to-all-start = ((bf16[8,16,512]{2,1,0:T(8,128)(2,1)}), bf16[8,16,512]{2,1,0:T(8,128)(2,1)S(1)}, u32[]{:S(2)}, u32[]{:S(2)}) async-start(bf16[8,16,512]{2,1,0:T(8,128)(2,1)} %broadcast_in_dim.4), calls=%async_computation | async-start | bytes 262144 | tf_op jit(solution)/shard_map/all_to_all | solution.py:140
  35.1 0.0 copy-done.1
  35.1 1.2 %convolution_convert_fusion = bf16[128,512]{1,0:T(8,128)(2,1)S(1)} fusion(f32[128,512]{1,0:T(8,128)S(1)} %copy-done.1, f32[512,512]{1,0:T(8,128)S(1)} %copy-done), kind=kOutput, calls=%fused_computation | convolution fusion | flops 402718720 | bytes 1441792 | tf_op jit(solution)/shard_map/dot_general | solution.py:36
  36.3 0.0 copy-start.2
  36.3 1.9 %collective-permute-start.6 = (bf16[128,512]{1,0:T(8,128)(2,1)S(1)}, bf16[128,512]{1,0:T(8,128)(2,1)S(1)}, u32[]{:S(2)}, u32[]{:S(2)}) collective-permute-start(bf16[128,512]{1,0:T(8,128)(2,1)S(1)} %convolution_convert_fusion), channel_id=1, source_target_pairs={{0,4},{1,5},{2,6},{3,7},{4,0},{5,1},{6,2},{7,3},{8,12},{9,13},{10,... | collective-permute-start | bytes 393224 | tf_op jit(solution)/shard_map/ppermute | solution.py:28
  38.2 1.9 %collective-permute-start.5 = (bf16[128,512]{1,0:T(8,128)(2,1)S(1)}, bf16[128,512]{1,0:T(8,128)(2,1)S(1)}, u32[]{:S(2)}, u32[]{:S(2)}) collective-permute-start(bf16[128,512]{1,0:T(8,128)(2,1)S(1)} %convolution_convert_fusion), channel_id=1, source_target_pairs={{0,2},{1,3},{2,0},{3,1},{4,6},{5,7},{6,4},{7,5},{8,10},{9,11},{10,... | collective-permute-start | bytes 393224 | tf_op jit(solution)/shard_map/ppermute | solution.py:28
  40.2 5.0 %collective-permute-done.6 = bf16[128,512]{1,0:T(8,128)(2,1)S(1)} collective-permute-done((bf16[128,512]{1,0:T(8,128)(2,1)S(1)}, bf16[128,512]{1,0:T(8,128)(2,1)S(1)}, u32[]{:S(2)}, u32[]{:S(2)}) %collective-permute-start.6) | collective-permute-done | bytes 131104 | tf_op jit(solution)/shard_map/ppermute | solution.py:28
  45.2 1.1 %collective-permute-done.5 = bf16[128,512]{1,0:T(8,128)(2,1)S(1)} collective-permute-done((bf16[128,512]{1,0:T(8,128)(2,1)S(1)}, bf16[128,512]{1,0:T(8,128)(2,1)S(1)}, u32[]{:S(2)}, u32[]{:S(2)}) %collective-permute-start.5) | collective-permute-done | bytes 131104 | tf_op jit(solution)/shard_map/ppermute | solution.py:28
  46.3 0.0 all-to-all-done
  46.3 1.1 %broadcast_in_dim.5 = bf16[8,8,16,512]{3,2,1,0:T(8,128)(2,1)} broadcast(bf16[8,16,512]{2,1,0:T(8,128)(2,1)S(1)} %all-to-all-done), dimensions={1,2,3} | broadcast | bytes 1179648 | tf_op jit(solution)/shard_map/broadcast_in_dim | solution.py:46
  47.4 3.6 %all-to-all-start.1 = ((bf16[8,8,16,512]{3,2,1,0:T(8,128)(2,1)}), bf16[8,8,16,512]{3,2,1,0:T(8,128)(2,1)S(1)}, u32[]{:S(2)}, u32[]{:S(2)}) async-start(bf16[8,8,16,512]{3,2,1,0:T(8,128)(2,1)} %broadcast_in_dim.5), calls=%async_computation.1 | async-start | bytes 2097152 | tf_op jit(solution)/shard_map/all_to_all | solution.py:47
  51.1 3.5 %collective-permute-start.7 = (bf16[128,512]{1,0:T(8,128)(2,1)S(1)}, bf16[128,512]{1,0:T(8,128)(2,1)S(1)}, u32[]{:S(2)}, u32[]{:S(2)}) collective-permute-start(bf16[128,512]{1,0:T(8,128)(2,1)S(1)} %convolution_convert_fusion), channel_id=1, source_target_pairs={{0,6},{1,7},{2,4},{3,5},{4,2},{5,3},{6,0},{7,1},{8,14},{9,15},{10,... | collective-permute-start | bytes 393224 | tf_op jit(solution)/shard_map/ppermute | solution.py:28
  54.6 4.8 %collective-permute-done.7 = bf16[128,512]{1,0:T(8,128)(2,1)S(1)} collective-permute-done((bf16[128,512]{1,0:T(8,128)(2,1)S(1)}, bf16[128,512]{1,0:T(8,128)(2,1)S(1)}, u32[]{:S(2)}, u32[]{:S(2)}) %collective-permute-start.7) | collective-permute-done | bytes 131104 | tf_op jit(solution)/shard_map/ppermute | solution.py:28
  59.4 0.1 pad_maximum_fusion.mine_ref
  59.5 0.0 copy-done.2
  59.5 1.9 %collective-permute-start.8 = (bf16[4,128,512]{2,1,0:T(8,128)(2,1)S(1)}, bf16[4,128,512]{2,1,0:T(8,128)(2,1)S(1)}, u32[]{:S(2)}, u32[]{:S(2)}) collective-permute-start(bf16[4,128,512]{2,1,0:T(8,128)(2,1)S(1)} %pad_maximum_fusion.mine_ref), channel_id=1, source_target_pairs={{0,1},{1,0},{2,3},{3,2},{4,5},{5,4},{6,7},{7,6},{8,9},{9,8},{10,11... | collective-permute-start | bytes 1572872 | tf_op jit(solution)/shard_map/ppermute | solution.py:28
  61.4 1.9 %collective-permute-done.8.other_ref = bf16[4,128,512]{2,1,0:T(8,128)(2,1)S(1)} collective-permute-done((bf16[4,128,512]{2,1,0:T(8,128)(2,1)S(1)}, bf16[4,128,512]{2,1,0:T(8,128)(2,1)S(1)}, u32[]{:S(2)}, u32[]{:S(2)}) %collective-permute-start.8) | collective-permute-done | bytes 524320 | tf_op jit(solution)/shard_map/ppermute | solution.py:28
  63.3 1.8 %all-to-all-done.1.near_ref = bf16[8,8,16,512]{3,2,1,0:T(8,128)(2,1)S(1)} async-done(((bf16[8,8,16,512]{3,2,1,0:T(8,128)(2,1)}), bf16[8,8,16,512]{3,2,1,0:T(8,128)(2,1)S(1)}, u32[]{:S(2)}, u32[]{:S(2)}) %all-to-all-start.1) | async-done | bytes 1048608 | tf_op jit(solution)/shard_map/all_to_all | solution.py:47
  65.1 3.6 %shard_map.50 = bf16[1024,1024]{1,0:T(8,128)(2,1)} custom-call(bf16[4,128,512]{2,1,0:T(8,128)(2,1)S(1)} %pad_maximum_fusion.mine_ref, bf16[4,128,512]{2,1,0:T(8,128)(2,1)S(1)} %collective-permute-done.8.other_ref, bf16[8,8,16,512]{3,2,1,0:T(8,128)(2,1)S(1)} %all-to-all-done.1.near_ref, bf16[1024,1024]{1,0:T(8,128)(2,1)} %slab_ref.1), custom_call_target="tpu_custom_call" | custom-call | flops 1073741824 | bytes 6291456 | tf_op jit(solution)/shard_map/pallas_call | solution.py:114
  (1 shorter events, 0.0 us)
Async XLA Ops:
  0.6 17.2 %copy-start = (f32[512,512]{1,0:T(8,128)S(1)}, f32[512,512]{1,0:T(8,128)}, u32[]{:S(2)}) copy-start(f32[512,512]{1,0:T(8,128)} %param.4) | copy-start | bytes 3145732
  0.6 34.5 %copy-start.1 = (f32[128,512]{1,0:T(8,128)S(1)}, f32[128,512]{1,0:T(8,128)}, u32[]{:S(2)}) copy-start(f32[128,512]{1,0:T(8,128)} %param.3) | copy-start | bytes 786436
  0.7 0.8 %collective-permute-start = (f32[128,512]{1,0:T(8,128)}, f32[128,512]{1,0:T(8,128)S(1)}, u32[]{:S(2)}, u32[]{:S(2)}) collective-permute-start(f32[128,512]{1,0:T(8,128)} %param.3), channel_id=1, source_target_pairs={{0,1},{8,9},{16,17},{24,25},{32,33},{40,41},{48,49},{56,57},{64,65... | collective-permute-start | bytes 786440 | tf_op jit(solution)/shard_map/ppermute | solution.py:28
  2.4 3.3 %collective-permute-start.2 = (f32[16,512]{1,0:T(8,128)S(1)}, f32[16,512]{1,0:T(8,128)S(1)}, u32[]{:S(2)}, u32[]{:S(2)}) collective-permute-start(f32[16,512]{1,0:T(8,128)S(1)} %get-tuple-element.14), channel_id=1, source_target_pairs={{0,8},{1,40},{8,9},{9,41},{16,10},{17,42},{24,11},{25,43},{32,12},... | collective-permute-start | bytes 98312 | tf_op jit(solution)/shard_map/ppermute | solution.py:28
  3.1 2.7 %collective-permute-start.4 = (f32[16,512]{1,0:T(8,128)S(1)}, f32[16,512]{1,0:T(8,128)S(1)}, u32[]{:S(2)}, u32[]{:S(2)}) collective-permute-start(f32[16,512]{1,0:T(8,128)S(1)} %get-tuple-element.15), channel_id=1, source_target_pairs={{0,24},{1,56},{8,25},{9,57},{16,26},{17,58},{24,27},{25,59},{32,28... | collective-permute-start | bytes 98312 | tf_op jit(solution)/shard_map/ppermute | solution.py:28
  3.8 2.0 %collective-permute-start.3 = (f32[16,512]{1,0:T(8,128)S(1)}, f32[16,512]{1,0:T(8,128)S(1)}, u32[]{:S(2)}, u32[]{:S(2)}) collective-permute-start(f32[16,512]{1,0:T(8,128)S(1)} %get-tuple-element.16), channel_id=1, source_target_pairs={{0,16},{1,48},{8,17},{9,49},{16,18},{17,50},{24,19},{25,51},{32,20... | collective-permute-start | bytes 98312 | tf_op jit(solution)/shard_map/ppermute | solution.py:28
  4.4 13.3 %collective-permute-start.1 = (f32[16,512]{1,0:T(8,128)S(1)}, f32[16,512]{1,0:T(8,128)S(1)}, u32[]{:S(2)}, u32[]{:S(2)}) collective-permute-start(f32[16,512]{1,0:T(8,128)S(1)} %get-tuple-element.17), channel_id=1, source_target_pairs={{0,0},{1,32},{8,1},{9,33},{16,2},{17,34},{24,3},{25,35},{32,4},{33... | collective-permute-start | bytes 98312 | tf_op jit(solution)/shard_map/ppermute | solution.py:28
  19.4 26.9 %all-to-all-start = ((bf16[8,16,512]{2,1,0:T(8,128)(2,1)}), bf16[8,16,512]{2,1,0:T(8,128)(2,1)S(1)}, u32[]{:S(2)}, u32[]{:S(2)}) async-start(bf16[8,16,512]{2,1,0:T(8,128)(2,1)} %broadcast_in_dim.4), calls=%async_computation | async-start | bytes 262144 | tf_op jit(solution)/shard_map/all_to_all | solution.py:140
  36.3 23.2 %copy-start.2 = (bf16[128,512]{1,0:T(8,128)(2,1)}, bf16[128,512]{1,0:T(8,128)(2,1)S(1)}, u32[]{:S(2)}) copy-start(bf16[128,512]{1,0:T(8,128)(2,1)S(1)} %convolution_convert_fusion) | copy-start | bytes 393220
  36.3 8.9 %collective-permute-start.6 = (bf16[128,512]{1,0:T(8,128)(2,1)S(1)}, bf16[128,512]{1,0:T(8,128)(2,1)S(1)}, u32[]{:S(2)}, u32[]{:S(2)}) collective-permute-start(bf16[128,512]{1,0:T(8,128)(2,1)S(1)} %convolution_convert_fusion), channel_id=1, source_target_pairs={{0,4},{1,5},{2,6},{3,7},{4,0},{5,1},{6,2},{7,3},{8,12},{9,13},{10,... | collective-permute-start | bytes 393224 | tf_op jit(solution)/shard_map/ppermute | solution.py:28
  38.2 8.1 %collective-permute-start.5 = (bf16[128,512]{1,0:T(8,128)(2,1)S(1)}, bf16[128,512]{1,0:T(8,128)(2,1)S(1)}, u32[]{:S(2)}, u32[]{:S(2)}) collective-permute-start(bf16[128,512]{1,0:T(8,128)(2,1)S(1)} %convolution_convert_fusion), channel_id=1, source_target_pairs={{0,2},{1,3},{2,0},{3,1},{4,6},{5,7},{6,4},{7,5},{8,10},{9,11},{10,... | collective-permute-start | bytes 393224 | tf_op jit(solution)/shard_map/ppermute | solution.py:28
  47.4 17.7 %all-to-all-start.1 = ((bf16[8,8,16,512]{3,2,1,0:T(8,128)(2,1)}), bf16[8,8,16,512]{3,2,1,0:T(8,128)(2,1)S(1)}, u32[]{:S(2)}, u32[]{:S(2)}) async-start(bf16[8,8,16,512]{3,2,1,0:T(8,128)(2,1)} %broadcast_in_dim.5), calls=%async_computation.1 | async-start | bytes 2097152 | tf_op jit(solution)/shard_map/all_to_all | solution.py:47
  51.1 8.4 %collective-permute-start.7 = (bf16[128,512]{1,0:T(8,128)(2,1)S(1)}, bf16[128,512]{1,0:T(8,128)(2,1)S(1)}, u32[]{:S(2)}, u32[]{:S(2)}) collective-permute-start(bf16[128,512]{1,0:T(8,128)(2,1)S(1)} %convolution_convert_fusion), channel_id=1, source_target_pairs={{0,6},{1,7},{2,4},{3,5},{4,2},{5,3},{6,0},{7,1},{8,14},{9,15},{10,... | collective-permute-start | bytes 393224 | tf_op jit(solution)/shard_map/ppermute | solution.py:28
  59.5 3.8 %collective-permute-start.8 = (bf16[4,128,512]{2,1,0:T(8,128)(2,1)S(1)}, bf16[4,128,512]{2,1,0:T(8,128)(2,1)S(1)}, u32[]{:S(2)}, u32[]{:S(2)}) collective-permute-start(bf16[4,128,512]{2,1,0:T(8,128)(2,1)S(1)} %pad_maximum_fusion.mine_ref), channel_id=1, source_target_pairs={{0,1},{1,0},{2,3},{3,2},{4,5},{5,4},{6,7},{7,6},{8,9},{9,8},{10,11... | collective-permute-start | bytes 1572872 | tf_op jit(solution)/shard_map/ppermute | solution.py:28
